TPU v7x, 128 devices: a whole 4x4x4 slice. The times are simulated.
128 devices in a mesh: row: 8 (over y_lo, z), col: 16 (over x, y_hi, core).
Axes of the slice: x: 4, y: 4 (y_hi: 2, y_lo: 2; y = y_hi * 2 + y_lo), z: 4, core: 2. Of those that a mesh axis runs over, the one named last changes fastest.
Arguments:
- hessian: float32 [16384, 8, 16, 128], P('row', None, 'col'), may hold values from -1 to 16, as said below
- weights: bfloat16 [512, 16384], P('col', 'row'), may hold values from -6 to 6
- codes: int32 [512, 8192], P('col', 'row'), may hold values from 0 to 255
- tile_map: int32 [32, 64], P('col', 'row'), may hold values from 0 to 511
- codebooks: float32 [512, 2, 256], replicated, may hold values from -6 to 6
Outputs:
- adjusted_codebooks: float32 [512, 2, 256], replicated
Inputs may be any that keep to these rules, and one draw needn't show every extreme that they name: `hessian`: H is symmetric with a dominant positive diagonal.
All inputs are finite; a program needn't handle non-finite values.
Results may differ from a plain program's by a relative error of at most 0.0003.
Values sent between devices are 32-bit elements; how exact they have to be, the bound alone decides.
No kernel may reach another device: no remote copies, remote signals or barrier semaphores. Data moves between devices by JAX's collectives and lax.ppermute only.
A program may use at most 64 MiB of HBM per device.

v0:
```python
import jax
import jax.numpy as jnp
from jax import lax
from jax.sharding import PartitionSpec as P

CODES = 256
NB = 512
TILE_ROWS = 16
TILE_COLS = 256
STEPS = 2


learn_rate = 0.01


def per_device(hessian, weights, codes, tile_map, codebooks):
    rows_local, cols_local = weights.shape
    rows_tiles = rows_local // TILE_ROWS
    cols_tiles = cols_local // TILE_COLS
    tile_count = rows_tiles * cols_tiles
    half_width = TILE_COLS // 2
    pair_count = TILE_ROWS * half_width
    hessian_tile = hessian.reshape(
        hessian.shape[0], hessian.shape[1] * hessian.shape[2] * hessian.shape[3]
    )
    code_tiles = (
        codes.reshape(rows_tiles, TILE_ROWS, cols_tiles, half_width)
        .transpose(0, 2, 1, 3)
        .reshape(tile_count, pair_count)
    )
    code_onehot = (
        code_tiles[:, :, None] == lax.broadcasted_iota(jnp.int32, (1, 1, CODES), 2)
    ).astype(jnp.float32)
    book_onehot = (
        tile_map.reshape(-1)[:, None] == lax.broadcasted_iota(jnp.int32, (1, NB), 1)
    ).astype(jnp.float32)
    for iteration in range(STEPS):
        tile_books = jnp.einsum(
            "tb,bck->tck", book_onehot, codebooks, precision=lax.Precision.HIGHEST
        )
        rebuilt_tiles = jnp.einsum(
            "tpk,tck->tpc", code_onehot, tile_books, precision=lax.Precision.HIGHEST
        )
        rebuilt = (
            rebuilt_tiles.reshape(rows_tiles, cols_tiles, TILE_ROWS, half_width, 2)
            .transpose(0, 2, 1, 3, 4)
            .reshape(rows_local, cols_local)
        )
        error = rebuilt - weights.astype(jnp.float32)
        gathered = lax.all_gather(error, "col", axis=0, tiled=True)
        piece_width = cols_local // lax.axis_size("col")
        error_piece = lax.dynamic_slice_in_dim(
            gathered, lax.axis_index("col") * piece_width, piece_width, 1
        )
        error_spread = lax.all_gather(error_piece, "row", axis=1, tiled=True)
        weight_grad = 2.0 * lax.psum_scatter(
            lax.dot_general(
                error_spread,
                hessian_tile,
                (((1,), (1,)), ((), ())),
                precision=lax.Precision.HIGHEST,
                preferred_element_type=jnp.float32,
            ),
            "col",
            scatter_dimension=0,
            tiled=True,
        )
        grad_tiles = (
            weight_grad.reshape(rows_tiles, TILE_ROWS, cols_tiles, half_width, 2)
            .transpose(0, 2, 1, 3, 4)
            .reshape(tile_count, pair_count, 2)
        )
        tile_grads = jnp.einsum(
            "tpk,tpc->tck", code_onehot, grad_tiles, precision=lax.Precision.HIGHEST
        )
        local_grad = jnp.einsum(
            "tb,tck->bck", book_onehot, tile_grads, precision=lax.Precision.HIGHEST
        )
        total_even, total_odd = lax.psum((local_grad[:, 0, :], local_grad[:, 1, :]), ("row", "col"))
        book_grad = jnp.stack([total_even, total_odd], axis=1)
        codebooks = codebooks - learn_rate * book_grad
    return codebooks


def solution(mesh):
    placed = (P("row", None, "col", None), P("col", "row"), P("col", "row"), P("col", "row"), P())
    return jax.shard_map(per_device, mesh=mesh, in_specs=placed, out_specs=P(), check_vma=False)
```

profile of v0, /device:TPU:1, one launch (start us, length us, event | category | flops | bytes accessed | tf_op | source)
XLA Modules:
  0.0 803.9 jit_solution(11324388309986088203)
XLA Ops:
  8.3 1.7 fusion.16
  10.0 17.1 %fusion.3 = f32[16,2048,2]{1,2,0:T(2,128)S(1)} fusion(s32[16,2048]{1,0:T(8,128)S(1)} %bitcast_bitcast_fusion, f32[16,2,256]{2,0,1:T(8,128)S(1)} %fusion.16), kind=kOutput, calls=%fused_computation.4 | convolution fusion | flops 209715200 | bytes 425984 | tf_op jit(solution)/shard_map/tpk,tck->tpc/dot_general | solution.py:41
  27.3 1.4 copy.39
  31.0 59.7 %all-gather.5.cloned.1.call-done = f32[512,2048]{1,0:T(8,128)} async-done(((f32[32,2048]{1,0:T(8,128)}), f32[512,2048]{1,0:T(8,128)}) %all-gather.5.cloned.1.call-update) | async-done | bytes 4194320 | tf_op jit(solution)/shard_map/all_gather | solution.py:50
  90.7 1.7 constant_dynamic-slice_fusion.1
  92.4 39.8 %all-gather.7.cloned.1.call-done = f32[512,1024]{1,0:T(8,128)} async-done(((f32[512,128]{1,0:T(8,128)}), f32[512,1024]{1,0:T(8,128)}) %all-gather.7.cloned.1.call-update) | async-done | bytes 2097168 | tf_op jit(solution)/shard_map/all_gather | solution.py:55
  132.2 19.4 %fusion.10 = f32[512,2048]{1,0:T(8,128)} fusion(f32[512,1024]{1,0:T(8,128)} %all-gather.7.cloned.1.call-done, f32[256,8,8,128]{3,2,1,0:T(8,128)} %bitcast.51), kind=kOutput, calls=%fused_computation.11 | convolution fusion | flops 12884901888 | bytes 14680064 | tf_op jit(solution)/shard_map/dot_general | solution.py:57
  151.8 84.1 %reduce-scatter.3.cloned.1.call-done = f32[32,2048]{1,0:T(8,128)} async-done(((f32[512,2048]{1,0:T(8,128)}), f32[32,2048]{1,0:T(8,128)}) %reduce-scatter.3.cloned.1.call-update) | async-done | bytes 262160 | tf_op jit(solution)/shard_map/reduce_scatter | solution.py:56
  239.4 12.3 %fusion.2 = f32[16,2,256]{2,1,0:T(2,128)S(1)} fusion(f32[16,2048,2]{1,2,0:T(2,128)S(1)} %reshape.47, s32[16,2048]{1,0:T(8,128)} %copy-done.4), kind=kOutput, calls=%fused_computation.3 | convolution fusion | flops 209715200 | bytes 425984 | tf_op jit(solution)/shard_map/tpk,tpc->tck/dot_general | solution.py:73
  253.5 148.0 %all-reduce.7.cloned.1.call-done = (f32[512,1,256]{2,0,1:T(8,128)}, f32[512,1,256]{2,0,1:T(8,128)}) async-done(((f32[512,1,256]{2,0,1:T(8,128)}, f32[512,1,256]{2,0,1:T(8,128)}), (f32[512,1,256]{2,0,1:T(8,128)}, f32[512,1,256]{2,0,1:T(8,128)})) %all-reduce.7.cloned.1.call-update) | async-done | bytes 1048592 | tf_op jit(solution)/shard_map/psum | solution.py:79
  401.6 1.7 fusion.18
  403.3 17.1 %fusion.1 = f32[16,2048,2]{1,2,0:T(2,128)S(1)} fusion(s32[16,2048]{1,0:T(8,128)S(1)} %copy-done.5, f32[16,2,256]{2,0,1:T(8,128)S(1)} %fusion.18), kind=kOutput, calls=%fused_computation.2 | convolution fusion | flops 209715200 | bytes 425984 | tf_op jit(solution)/shard_map/tpk,tck->tpc/dot_general | solution.py:41
  422.0 2.1 reshape.39
  424.1 1.5 copy.48
  426.4 55.1 %all-gather.9.cloned.1.call-done = f32[512,2048]{1,0:T(8,128)} async-done(((f32[32,2048]{1,0:T(8,128)}), f32[512,2048]{1,0:T(8,128)}) %all-gather.9.cloned.1.call-update) | async-done | bytes 4194320 | tf_op jit(solution)/shard_map/all_gather | solution.py:50
  481.6 1.7 constant_dynamic-slice_fusion
  483.6 39.5 %all-gather.11.cloned.1.call-done = f32[512,1024]{1,0:T(8,128)} async-done(((f32[512,128]{1,0:T(8,128)}), f32[512,1024]{1,0:T(8,128)}) %all-gather.11.cloned.1.call-update) | async-done | bytes 2097168 | tf_op jit(solution)/shard_map/all_gather | solution.py:55
  523.1 19.4 %fusion.8 = f32[512,2048]{1,0:T(8,128)} fusion(f32[512,1024]{1,0:T(8,128)} %all-gather.11.cloned.1.call-done, f32[256,8,8,128]{3,2,1,0:T(8,128)} %bitcast.52), kind=kOutput, calls=%fused_computation.9 | convolution fusion | flops 12884901888 | bytes 14680064 | tf_op jit(solution)/shard_map/dot_general | solution.py:57
  542.8 84.0 %reduce-scatter.5.cloned.1.call-done = f32[32,2048]{1,0:T(8,128)} async-done(((f32[512,2048]{1,0:T(8,128)}), f32[32,2048]{1,0:T(8,128)}) %reduce-scatter.5.cloned.1.call-update) | async-done | bytes 262160 | tf_op jit(solution)/shard_map/reduce_scatter | solution.py:56
  629.2 2.5 reshape.40
  632.7 11.3 %fusion = f32[16,2,256]{2,1,0:T(2,128)S(1)} fusion(f32[16,2048,2]{1,2,0:T(2,128)S(1)} %reshape.48, s32[16,2048]{1,0:T(8,128)S(1)} %copy-done.6), kind=kOutput, calls=%fused_computation.1 | convolution fusion | flops 209715200 | bytes 425984 | tf_op jit(solution)/shard_map/tpk,tpc->tck/dot_general | solution.py:73
  645.7 148.1 %all-reduce.5.cloned.1.call-done = (f32[512,1,256]{2,0,1:T(8,128)}, f32[512,1,256]{2,0,1:T(8,128)}) async-done(((f32[512,1,256]{2,0,1:T(8,128)}, f32[512,1,256]{2,0,1:T(8,128)}), (f32[512,1,256]{2,0,1:T(8,128)}, f32[512,1,256]{2,0,1:T(8,128)})) %all-reduce.5.cloned.1.call-update) | async-done | bytes 1048592 | tf_op jit(solution)/shard_map/psum | solution.py:79
  793.9 1.4 fusion.15
  795.3 1.8 copy.53
  (53 shorter events, 17.7 us)
Async XLA Ops:
  6.5 84.1 %all-gather.5.cloned.1.call-start = ((), (), s32[]{:S(2)}) async-start(), calls=%async_computation.2 | async-start | bytes 4456448 | tf_op jit(solution)/shard_map/all_gather | solution.py:50
  8.2 1.7 copy-start.4
  10.0 20.2 %copy-start.3 = (bf16[32,2048]{1,0:T(8,128)(2,1)S(1)}, bf16[32,2048]{1,0:T(8,128)(2,1)}, u32[]{:S(2)}) copy-start(bf16[32,2048]{1,0:T(8,128)(2,1)} %param.6) | copy-start | bytes 393220
  30.9 101.3 %all-gather.7.cloned.1.call-start = ((), (), s32[]{:S(2)}) async-start(), calls=%async_computation.3 | async-start | bytes 2359296 | tf_op jit(solution)/shard_map/all_gather | solution.py:55
  92.4 143.6 %reduce-scatter.3.cloned.1.call-start = ((), (), s32[]{:S(2)}) async-start(), calls=%async_computation.4 | async-start | bytes 4456448 | tf_op jit(solution)/shard_map/reduce_scatter | solution.py:56
  151.6 250.0 %all-reduce.7.cloned.1.call-start = ((), (), s32[]{:S(2)}) async-start(), calls=%async_computation.9 | async-start | bytes 2097152 | tf_op jit(solution)/shard_map/psum | solution.py:79
  239.2 162.3 %copy-start = (f32[512,2,256]{2,1,0:T(2,128)S(1)}, f32[512,2,256]{2,1,0:T(2,128)}, u32[]{:S(2)}) copy-start(f32[512,2,256]{2,1,0:T(2,128)} %param.9) | copy-start | bytes 3145732
  239.4 163.9 %copy-start.5 = (s32[16,2048]{1,0:T(8,128)S(1)}, s32[16,2048]{1,0:T(8,128)}, u32[]{:S(2)}) copy-start(s32[16,2048]{1,0:T(8,128)} %copy-done.4) | copy-start | bytes 393220
  253.5 228.1 %all-gather.9.cloned.1.call-start = ((), (), s32[]{:S(2)}) async-start(), calls=%async_computation.5 | async-start | bytes 4456448 | tf_op jit(solution)/shard_map/all_gather | solution.py:50
  426.4 96.7 %all-gather.11.cloned.1.call-start = ((), (), s32[]{:S(2)}) async-start(), calls=%async_computation.6 | async-start | bytes 2359296 | tf_op jit(solution)/shard_map/all_gather | solution.py:55
  483.3 143.6 %reduce-scatter.5.cloned.1.call-start = ((), (), s32[]{:S(2)}) async-start(), calls=%async_computation.7 | async-start | bytes 4456448 | tf_op jit(solution)/shard_map/reduce_scatter | solution.py:56
  542.5 90.2 %copy-start.6 = (s32[16,2048]{1,0:T(8,128)S(1)}, s32[16,2048]{1,0:T(8,128)}, u32[]{:S(2)}) copy-start(s32[16,2048]{1,0:T(8,128)} %copy-done.4) | copy-start | bytes 393220
  542.5 251.3 %all-reduce.5.cloned.1.call-start = ((), (), s32[]{:S(2)}) async-start(), calls=%async_computation.8 | async-start | bytes 2097152 | tf_op jit(solution)/shard_map/psum | solution.py:79
  632.5 161.4 %copy-start.1 = (f32[512,1,256]{2,0,1:T(8,128)S(1)}, f32[512,1,256]{2,0,1:T(8,128)}, u32[]{:S(2)}) copy-start(f32[512,1,256]{2,0,1:T(8,128)} %get-tuple-element.7) | copy-start | bytes 1572868
  632.5 161.4 %copy-start.2 = (f32[512,1,256]{2,0,1:T(8,128)S(1)}, f32[512,1,256]{2,0,1:T(8,128)}, u32[]{:S(2)}) copy-start(f32[512,1,256]{2,0,1:T(8,128)} %get-tuple-element.8) | copy-start | bytes 1572868
Sparse Core Ops, SparseCore 0:
  31.0 59.5 all-gather.4
  92.5 39.6 all-gather.6
  151.7 84.1 reduce-scatter.2
  253.6 147.8 all-reduce.6
  426.5 55.0 all-gather.8
  483.4 39.6 all-gather.10
  542.6 84.1 reduce-scatter.4
  645.9 147.9 all-reduce.4
where the time goes:
time: 804 us
  waiting for transfers between devices  659 us (82%)
  matrix products  101 us (13%)
  local copies, waits for them, and re-layouts  24.4 us (3%)
  between operations  13.7 us (2%)
    psum x2, waiting for transfers between devices, per_device(): lax.psum((local_grad[:, 0, :], local_grad[:, 1, :]), ('row', 'col'))  296 us
    reduce_scatter x2, waiting for transfers between devices, per_device(): lax.psum_scatter(lax.dot_general(error_spread, hessian_tile, (((1,), (1,)...  168 us
    all_gather x2, waiting for transfers between devices, per_device(): gathered = lax.all_gather(error, 'col', axis=0, tiled=True)  115 us
    all_gather x2, waiting for transfers between devices, per_device(): error_spread = lax.all_gather(error_piece, 'row', axis=1, tiled=True)  79.3 us
    dot_general x2, matrix products, per_device(): lax.dot_general(error_spread, hessian_tile, (((1,), (1,)), ((), ())), pre...  38.8 us
    dot_general x2, matrix products, per_device(): jnp.einsum('tpk,tck->tpc', code_onehot, tile_books, precision=lax.Precisi...  34.2 us
    dot_general x2, matrix products, per_device(): jnp.einsum('tpk,tpc->tck', code_onehot, grad_tiles, precision=lax.Precisi...  23.6 us
  transfers between devices with their start and end apart: 8, of which 8 were waited for; matrix products, arithmetic and copies ran while one was open for 0% of the time, Pallas kernels for 0%

commit v1 on v0

v1 whole, which is shorter than its diff:
```python
import jax
import jax.numpy as jnp
from jax import lax
from jax.experimental import pallas as pl
from jax.experimental.pallas import tpu as pltpu
from jax.sharding import PartitionSpec as P

F32 = jnp.float32
BF16 = jnp.bfloat16
I32 = jnp.int32
LEARN_RATE = 0.01
BOTH = ("row", "col")
VMEM_LIMIT = 56 * 1024 * 1024


def partners(dx, dyh, dcore, dyl, dz):
    flip_col = dx * 4 + dyh * 2 + dcore
    flip_row = dyl * 4 + dz
    return [(i, i ^ (flip_row * 16 + flip_col)) for i in range(128)]


def swap(v, dx=0, dyh=0, dcore=0, dyl=0, dz=0):
    return lax.ppermute(v, BOTH, partners(dx, dyh, dcore, dyl, dz))


def lanes(x, index):
    return jnp.take_along_axis(x, index, axis=1, mode="promise_in_bounds")


def iota(shape, dim):
    return lax.broadcasted_iota(I32, shape, dim)


def split(x):
    high = x.astype(BF16)
    low = (x - high.astype(F32)).astype(BF16)
    return high, low


def dot_nt(a, b):
    return lax.dot_general(a, b, (((1,), (1,)), ((), ())), preferred_element_type=F32)


def dot_nn(a, b):
    return lax.dot_general(a, b, (((1,), (0,)), ((), ())), preferred_element_type=F32)


def pick(index, even0, even1, odd0, odd1, odd):
    low = index & 127
    upper = index >= 128
    even_value = jnp.where(upper, lanes(even1, low), lanes(even0, low))
    odd_value = jnp.where(upper, lanes(odd1, low), lanes(odd0, low))
    return jnp.where(odd, odd_value, even_value)


def first_kernel(tile_ref, weights_ref, codes_ref, books_ref, error_ref, piece_ref, own_ref):
    lane = iota((16, 128), 1)
    odd = (lane & 1) == 1
    for q in range(8):
        codes = [codes_ref[t * 16 : t * 16 + 16, q * 128 : q * 128 + 128] for t in range(2)]
        books = [books_ref[tile_ref[t, q]] for t in range(2)]
        for h in range(2):
            piece = 2 * q + h
            for t in range(2):
                tables = [
                    jnp.broadcast_to(books[t][c : c + 1, k * 128 : k * 128 + 128], (16, 128))
                    for c in range(2)
                    for k in range(2)
                ]
                index = lanes(codes[t], h * 64 + (lane >> 1))
                value = pick(index, *tables, odd)
                weight = weights_ref[t * 16 : t * 16 + 16, piece * 128 : piece * 128 + 128]
                error_ref[piece, t * 16 : t * 16 + 16, :] = value - weight.astype(F32)
            place = h * 64 + (lane & 63)
            piece_ref[piece, 0:16, :] = jnp.where(lane < 64, lanes(codes[0], place), lanes(codes[1], place))
            piece_ref[piece, 16:24, :] = jnp.where(iota((8, 128), 1) == 0, tile_ref[0, q], tile_ref[1, q])
    own_ref[0:32, :] = codes_ref[...]
    wide = iota((8, 1024), 1)
    for t in range(2):
        row = jnp.zeros((8, 1024), I32)
        for q in range(8):
            row = jnp.where(wide == q, tile_ref[t, q], row)
        if t == 0:
            kept = row
    own_ref[32:40, :] = jnp.where(iota((8, 1024), 0) == 0, kept, row)


def first(weights, codes, tile_map, codebooks):
    vmem = pl.BlockSpec(memory_space=pltpu.VMEM)
    return pl.pallas_call(
        first_kernel,
        out_shape=[
            jax.ShapeDtypeStruct((16, 32, 128), F32),
            jax.ShapeDtypeStruct((16, 24, 128), I32),
            jax.ShapeDtypeStruct((40, 1024), I32),
        ],
        in_specs=[pl.BlockSpec(memory_space=pltpu.SMEM), vmem, vmem, vmem],
        out_specs=[vmem, vmem, vmem],
    )(tile_map, weights, codes, codebooks)


def sort_kernel(col_ref, near_ref, far_ref, packed_ref, rows_ref, keys_ref):
    col = col_ref[0]
    for core, part_ref in ((0, near_ref), (1, far_ref)):
        for m in range(8):
            where_to = (2 * m + core) ^ col
            rows_ref[pl.ds(pl.multiple_of(where_to * 40, 8), 40), :] = part_ref[m]
    for r in range(16):
        for t in range(2):
            keys_ref[(r * 2 + t) * 16 : (r * 2 + t) * 16 + 16, :] = rows_ref[pl.ds(t * 16 + r, 16, stride=40), :]
    size = 64
    lane = iota((size, 128), 1)

    def chunk(n, carry):
        start = pl.multiple_of(n * size, size)
        key = (keys_ref[pl.ds(start, size), :] * 128 + lane).astype(F32)
        k = 2
        while k <= 128:
            j = k // 2
            while j >= 1:
                other = lanes(key, lane ^ j)
                rising = ((lane & k) == 0) == ((lane & j) == 0)
                key = jnp.where(rising, jnp.minimum(key, other), jnp.maximum(key, other))
                j //= 2
            k *= 2
        whole = key.astype(I32)
        packed = whole & 127
        for half in range(2):
            limit = (half * 128 + lane + 1) * 128
            count = jnp.zeros((size, 128), I32)
            for step in (64, 32, 16, 8, 4, 2, 1, 1):
                below = lanes(whole, count + (step - 1)) < limit
                count = jnp.where(below, count + step, count)
            packed = packed | (count << (8 + 8 * half))
        packed_ref[pl.ds(start, size), :] = packed
        return carry

    lax.fori_loop(0, 512 // size, chunk, 0)


def sort_codes(col, near, far):
    block = pl.BlockSpec((8, 40, 128), lambda q: (0, 0, q))
    return pl.pallas_call(
        sort_kernel,
        out_shape=jax.ShapeDtypeStruct((512, 1024), I32),
        grid=(8,),
        in_specs=[pl.BlockSpec(memory_space=pltpu.SMEM), block, block],
        out_specs=pl.BlockSpec((512, 128), lambda q: (0, q)),
        scratch_shapes=[pltpu.VMEM((640, 128), I32), pltpu.VMEM((512, 128), I32)],
    )(col, near, far)


def step_body(second, place_ref, hessian_ref, packed_ref, book_row_ref, refs):
    if second:
        (error_ref, piece_ref, near_ref, far_ref, book_col_ref), outs = refs[:5], refs[5:]
    else:
        (error_ref,), outs = refs[:1], refs[1:]
    keep_ref, send_ref, eh_ref, el_ref, hh_ref, hl_ref, sums_ref, table_ref = outs
    q = pl.program_id(0)
    place = place_ref[0]
    lane16 = iota((16, 128), 1)
    odd = (lane16 & 1) == 1

    @pl.when(q == 0)
    def _():
        if second:
            chosen = jnp.where((book_col_ref[...] ^ place) == iota((256, 512), 1), 1.0, 0.0).astype(BF16)
            total = jnp.zeros((256, 512), F32)
            for part, ref in ((0, near_ref), (1, far_ref)):
                high, low = split(ref[...])
                here = chosen[:, part * 256 : part * 256 + 256]
                total = total + dot_nn(here, high) + dot_nn(here, low)
            table_ref[...] = total

        def column(j, carry):
            if second:
                base = pl.multiple_of(j * 32, 32)
                tables = [
                    [table_ref[pl.ds(base + t * 16, 16), k * 128 : k * 128 + 128] for k in range(4)] for t in range(2)
                ]
            for r in range(16):
                if second:
                    codes = piece_ref[pl.ds(j * 384 + r, 16, stride=24), :]
                for t in range(2):
                    value = error_ref[pl.ds(j * 512 + t * 16 + r, 16, stride=32), :]
                    if second:
                        index = lanes(codes, t * 64 + (lane16 >> 1))
                        value = value - LEARN_RATE * pick(index, *tables[t], odd)
                    high, low = split(value)
                    rows = slice((r * 2 + t) * 16, (r * 2 + t) * 16 + 16)
                    eh_ref[j, rows, :] = high
                    el_ref[j, rows, :] = low
            return carry

        lax.fori_loop(0, 8, column, 0)

    for j in range(8):
        for parity in range(2):
            high, low = split(hessian_ref[pl.ds(parity * 8 + j, 128, stride=16), :])
            hh_ref[parity * 128 : parity * 128 + 128, j * 128 : j * 128 + 128] = high
            hl_ref[parity * 128 : parity * 128 + 128, j * 128 : j * 128 + 128] = low
    grad = jnp.zeros((512, 256), F32)
    for j in range(8):
        cut = slice(j * 128, j * 128 + 128)
        grad = grad + dot_nt(eh_ref[j], hh_ref[:, cut]) + dot_nt(el_ref[j], hh_ref[:, cut]) + dot_nt(eh_ref[j], hl_ref[:, cut])
    packed = packed_ref[...]
    source = packed & 127
    counts = [(packed >> 8) & 255, packed >> 16]
    running = jnp.where((iota((256, 128), 0) & 127) <= iota((256, 128), 1), 1.0, 0.0).astype(BF16)
    lane32 = iota((32, 128), 1)
    for c in range(2):
        ordered = lanes(grad[:, c * 128 : c * 128 + 128], source)
        prefix = dot_nn(jnp.concatenate(split(ordered), axis=1), running)
        upto = []
        for count in counts:
            value = jnp.where(count > 0, lanes(prefix, jnp.maximum(count - 1, 0)), 0.0)
            upto.append(value.reshape(16, 32, 128).sum(axis=0))
        before = [pltpu.roll(v, 1, 1) for v in upto]
        sums_ref[q, :, c * 256 : c * 256 + 128] = 2.0 * (upto[0] - jnp.where(lane32 == 0, 0.0, before[0]))
        sums_ref[q, :, c * 256 + 128 : c * 256 + 256] = 2.0 * (upto[1] - jnp.where(lane32 == 0, before[0], before[1]))

    @pl.when(q == 7)
    def _():
        chosen = jnp.where((iota((512, 256), 0) ^ place) == book_row_ref[...], 1.0, 0.0).astype(BF16)
        high, low = split(sums_ref[...].reshape(256, 512))
        total = dot_nn(chosen, high) + dot_nn(chosen, low)
        keep_ref[...] = total[0:256]
        send_ref[...] = total[256:512]


def step(second, place, hessian, packed, book_row, *rest):
    def kernel(place_ref, hessian_ref, packed_ref, book_row_ref, *refs):
        step_body(second, place_ref, hessian_ref, packed_ref, book_row_ref, refs)

    def whole(x):
        return pl.BlockSpec(x.shape, lambda q: (0,) * x.ndim)

    half = jax.ShapeDtypeStruct((256, 512), F32)
    return pl.pallas_call(
        kernel,
        out_shape=[half, half],
        grid=(8,),
        in_specs=[
            pl.BlockSpec(memory_space=pltpu.SMEM),
            pl.BlockSpec((2048, 128), lambda q: (q, 0)),
            pl.BlockSpec((512, 128), lambda q: (0, q)),
            whole(book_row),
        ]
        + [whole(x) for x in rest],
        out_specs=[pl.BlockSpec((256, 512), lambda q: (0, 0))] * 2,
        scratch_shapes=[
            pltpu.VMEM((8, 512, 128), BF16),
            pltpu.VMEM((8, 512, 128), BF16),
            pltpu.VMEM((256, 1024), BF16),
            pltpu.VMEM((256, 1024), BF16),
            pltpu.VMEM((8, 32, 512), F32),
            pltpu.VMEM((256, 512), F32),
        ],
        compiler_params=pltpu.CompilerParams(vmem_limit_bytes=VMEM_LIMIT),
    )(place, hessian, packed, book_row, *rest)


def last_kernel(place_ref, books_ref, near0_ref, far0_ref, near1_ref, far1_ref, out_ref):
    place = place_ref[0]
    for part, (a_ref, b_ref) in enumerate(((near0_ref, near1_ref), (far0_ref, far1_ref))):
        for k in range(4):
            start = pl.multiple_of((part * 256 + k * 64) ^ place, 64)
            for c in range(2):
                cut = (slice(k * 64, k * 64 + 64), slice(c * 256, c * 256 + 256))
                moved = LEARN_RATE * (a_ref[cut] + b_ref[cut])
                out_ref[pl.ds(start, 64), c, :] = books_ref[pl.ds(start, 64), c, :] - moved


def last(place, codebooks, *parts):
    vmem = pl.BlockSpec(memory_space=pltpu.VMEM)
    return pl.pallas_call(
        last_kernel,
        out_shape=jax.ShapeDtypeStruct((512, 2, 256), F32),
        in_specs=[pl.BlockSpec(memory_space=pltpu.SMEM)] + [vmem] * 5,
        out_specs=vmem,
    )(place, codebooks, *parts)


def sum_all(keep, send):
    half = keep + swap(send, dcore=1)
    quarter = [half[k * 64 : k * 64 + 64] for k in range(4)]
    got = [None] + [swap(quarter[k], dx=k) for k in (1, 2, 3)]
    s = (quarter[0] + got[2]) + (got[1] + got[3])
    got = [None] + [swap(s, dyl=k & 1, dyh=k >> 1) for k in (1, 2, 3)]
    s = (s + got[2]) + (got[1] + got[3])
    got = [None] + [swap(s, dz=k) for k in (1, 2, 3)]
    s = (s + got[2]) + (got[1] + got[3])
    near = jnp.concatenate([s] + [swap(s, dx=k) for k in (1, 2, 3)])
    return near, swap(near, dcore=1)


def per_device(hessian, weights, codes, tile_map, codebooks):
    col = lax.axis_index("col").astype(I32)
    place = ((col & 1) * 256 + (col >> 2) * 64).reshape(1)
    rows = hessian.reshape(16384, 128)
    error, piece, own = first(weights, codes, tile_map, codebooks)

    pair = jnp.stack([own, swap(own, dyh=1)])
    near = jnp.concatenate([pair] + [swap(pair, dx=k) for k in (1, 2, 3)])
    far = swap(near, dcore=1)
    packed = sort_codes(col.reshape(1), near, far)
    tiles = jnp.stack([near[:, 32:34, 0:8], far[:, 32:34, 0:8]], axis=1).reshape(16, 2, 8)
    same = (iota((16, 16), 0) ^ col) == iota((16, 16), 1)
    tiles = jnp.where(same[:, :, None, None], tiles[None], 0).sum(axis=1)
    book_row = tiles.transpose(2, 1, 0).reshape(1, 256)

    def spread(x):
        wide = jnp.broadcast_to(x[None], (8,) + x.shape).reshape((128,) + x.shape[1:])
        return lax.all_to_all(wide, BOTH, 0, 0, tiled=True)

    errors = spread(error).reshape(4096, 128)
    pieces = spread(piece)
    book_col = pieces.reshape(8, 16, 24, 128)[:, :, 16, 0:2].transpose(0, 2, 1).reshape(256, 1)
    pieces = pieces.reshape(3072, 128)

    near0, far0 = sum_all(*step(False, place, rows, packed, book_row, errors))
    near1, far1 = sum_all(*step(True, place, rows, packed, book_row, errors, pieces, near0, far0, book_col))
    return last(place, codebooks, near0, far0, near1, far1)


def solution(mesh):
    placed = (P("row", None, "col", None), P("col", "row"), P("col", "row"), P("col", "row"), P())
    return jax.shard_map(per_device, mesh=mesh, in_specs=placed, out_specs=P(), check_vma=False)
```

time: 804 us -> 431 us (0.54)
  waiting for transfers between devices: 659 us -> 90.6 us
  Pallas kernels: 0 us -> 257 us
  matrix products: 101 us -> 0 us
  starting transfers between devices: 0.96 us -> 67.3 us
  between operations: 13.7 us -> 0.24 us
  local copies, waits for them, and re-layouts: 24.4 us -> 12.2 us
    psum x2 -> x0, waiting for transfers between devices: 296 us -> none  [per_device(): lax.psum((local_grad[:, 0, :], local_grad[:, 1, :]), ('row', 'col'))]
    pallas_call x0 -> x5, Pallas kernels: none -> 257 us  [the longest x1 167 us: sort_codes(): pl.pallas_call(sort_kernel, out_shape=jax.ShapeDtypeStruct((512, 1024), I...]
    all_gather x4 -> x0, waiting for transfers between devices: 194 us -> none  [the longest x2 115 us: per_device(): gathered = lax.all_gather(error, 'col', axis=0, tiled=True)]
    reduce_scatter x2 -> x0, waiting for transfers between devices: 168 us -> none  [per_device(): lax.psum_scatter(lax.dot_general(error_spread, hessian_tile, (((1,), (1,)...]
    dot_general x10 -> x0, matrix products: 101 us -> none  [the longest x2 38.8 us: per_device(): lax.dot_general(error_spread, hessian_tile, (((1,), (1,)), ((), ())), pre...]
    ppermute x0 -> x33, waiting for transfers between devices: none -> 90.6 us  [swap(): return lax.ppermute(v, BOTH, partners(dx, dyh, dcore, dyl, dz))]
    ppermute x0 -> x33, starting transfers between devices: none -> 49.8 us  [swap(): return lax.ppermute(v, BOTH, partners(dx, dyh, dcore, dyl, dz))]
    all_to_all x0 -> x2, starting transfers between devices: none -> 17.4 us  [spread(): return lax.all_to_all(wide, BOTH, 0, 0, tiled=True)]
  transfers between devices with their start and end apart: 8 -> 35, of which waited for: 8 -> 25; matrix products, arithmetic and copies ran while one was open for 0% -> 2% of each run, Pallas kernels for 0% -> 39%
where the time goes in v1:
time: 431 us; the launch traced here: 430 us
  Pallas kernels  257 us (60%)
  waiting for transfers between devices  90.6 us (21%)
  starting transfers between devices  67.3 us (16%)
  local copies, waits for them, and re-layouts  12.2 us (3%)
    pallas_call x1, Pallas kernels, sort_codes(): pl.pallas_call(sort_kernel, out_shape=jax.ShapeDtypeStruct((512, 1024), I...  167 us
    ppermute x33, waiting for transfers between devices, swap(): return lax.ppermute(v, BOTH, partners(dx, dyh, dcore, dyl, dz))  90.6 us
    pallas_call x2, Pallas kernels, step(): pl.pallas_call(kernel, out_shape=[half, half], grid=(8,), in_specs=[pl.Bl...  81.9 us
    ppermute x33, starting transfers between devices, swap(): return lax.ppermute(v, BOTH, partners(dx, dyh, dcore, dyl, dz))  49.8 us
    all_to_all x2, starting transfers between devices, spread(): return lax.all_to_all(wide, BOTH, 0, 0, tiled=True)  17.4 us
  transfers between devices with their start and end apart: 35, of which 25 were waited for; matrix products, arithmetic and copies ran while one was open for 2% of the time, Pallas kernels for 39%

profile of v1, /device:TPU:1, one launch (start us, length us, event | category | flops | bytes accessed | tf_op | source)
XLA Modules:
  0.0 430.5 jit_solution(15722433418672112875)
XLA Ops:
  0.0 4.8 %shard_map.55 = (f32[16,32,128]{2,1,0:T(8,128)}, s32[16,24,128]{2,1,0:T(8,128)}, s32[40,1024]{1,0:T(8,128)}) custom-call(s32[2,8]{1,0:T(2,128)} %tile_ref.1, bf16[32,2048]{1,0:T(8,128)(2,1)} %weights_ref.1, s32[32,1024]{1,0:T(8,128)} %codes_ref.1, f32[512,2,256]{2,1,0:T(2,128)} %books_ref.3), custom_call_target="tpu_custom_call" | custom-call | tf_op jit(solution)/shard_map/pallas_call | solution.py:90
  4.8 3.7 collective-permute-start
  11.1 8.8 %all-to-all-start = ((f32[128,32,128]{2,1,0:T(8,128)}), f32[128,32,128]{2,1,0:T(8,128)S(1)}, u32[]{:S(2)}, u32[]{:S(2)}) async-start(f32[128,32,128]{2,1,0:T(8,128)} %bitcast.27), calls=%async_computation | async-start | bytes 4194304 | tf_op jit(solution)/shard_map/all_to_all | solution.py:314
  26.4 24.5 %collective-permute-done.1 = s32[2,40,1024]{2,1,0:T(8,128)S(1)} collective-permute-done((s32[2,40,1024]{2,1,0:T(8,128)S(1)}, s32[2,40,1024]{2,1,0:T(8,128)S(1)}, u32[]{:S(2)}, u32[]{:S(2)}) %collective-permute-start.1) | collective-permute-done | bytes 327712 | tf_op jit(solution)/shard_map/ppermute | solution.py:23
  50.9 8.5 %collective-permute-done.2 = s32[2,40,1024]{2,1,0:T(8,128)S(1)} collective-permute-done((s32[2,40,1024]{2,1,0:T(8,128)S(1)}, s32[2,40,1024]{2,1,0:T(8,128)S(1)}, u32[]{:S(2)}, u32[]{:S(2)}) %collective-permute-start.2) | collective-permute-done | bytes 327712 | tf_op jit(solution)/shard_map/ppermute | solution.py:23
  60.5 2.7 collective-permute-done.4.far_ref
  65.5 166.8 %shard_map.56.packed_ref = s32[512,1024]{1,0:T(8,128)} custom-call(s32[1]{0:T(128)} %bitcast.2.col_ref, s32[8,40,1024]{2,1,0:T(8,128)} %copy-done.5, s32[8,40,1024]{2,1,0:T(8,128)} %collective-permute-done.4.far_ref), custom_call_target="tpu_custom_call" | custom-call | tf_op jit(solution)/shard_map/pallas_call | solution.py:143
  233.5 31.5 %shard_map.57 = (f32[256,512]{1,0:T(8,128)}, f32[256,512]{1,0:T(8,128)}) custom-call(s32[1]{0:T(128)} %bitcast.place_ref, f32[16384,128]{1,0:T(8,128)} %bitcast.23, s32[512,1024]{1,0:T(8,128)} %shard_map.56.packed_ref, s32[1,256]{1,0:T(1,128)} %reshape.53.book_row_ref, f32[4096,128]{1,0:T(8,128)} %bitcast.25), custom_call_target="tpu_custom_call" | custom-call | tf_op jit(solution)/shard_map/pallas_call | solution.py:239
  269.3 3.0 collective-permute-start.6
  273.5 8.6 %all-to-all-start.1 = ((s32[128,24,128]{2,1,0:T(8,128)}), s32[128,24,128]{2,1,0:T(8,128)S(1)}, u32[]{:S(2)}, u32[]{:S(2)}) async-start(s32[128,24,128]{2,1,0:T(8,128)} %bitcast.11), calls=%async_computation.1 | async-start | bytes 3145728 | tf_op jit(solution)/shard_map/all_to_all | solution.py:314
  282.2 2.7 collective-permute-start.11
  286.2 18.4 %collective-permute-done.11 = f32[64,512]{1,0:T(8,128)S(1)} collective-permute-done((f32[64,512]{1,0:T(8,128)S(1)}, f32[64,512]{1,0:T(8,128)S(1)}, u32[]{:S(2)}, u32[]{:S(2)}) %collective-permute-start.11) | collective-permute-done | bytes 131104 | tf_op jit(solution)/shard_map/ppermute | solution.py:23
  304.6 3.0 collective-permute-done.9
  307.7 3.3 collective-permute-start.14
  315.0 3.0 collective-permute-done.12
  318.0 2.8 collective-permute-start.17
  321.5 4.4 %collective-permute-done.17 = f32[64,512]{1,0:T(8,128)S(1)} collective-permute-done((f32[64,512]{1,0:T(8,128)S(1)}, f32[64,512]{1,0:T(8,128)S(1)}, u32[]{:S(2)}, u32[]{:S(2)}) %collective-permute-start.17) | collective-permute-done | bytes 131104 | tf_op jit(solution)/shard_map/ppermute | solution.py:23
  326.3 3.5 collective-permute-start.18
  332.1 50.4 %shard_map.58 = (f32[256,512]{1,0:T(8,128)}, f32[256,512]{1,0:T(8,128)}) custom-call(s32[1]{0:T(128)} %bitcast.place_ref, f32[16384,128]{1,0:T(8,128)} %bitcast.24, s32[512,1024]{1,0:T(8,128)} %shard_map.56.packed_ref, s32[1,256]{1,0:T(1,128)} %reshape.53.book_row_ref, f32[4096,128]{1,0:T(8,128)} %bitcast.26, s32[3072,128]{1,0:T(8,128)} %bitcast.29, ...), custom_call_target="tpu_custom_call" | custom-call | tf_op jit(solution)/shard_map/pallas_call | solution.py:239
  392.0 3.5 collective-permute-done.20
  396.4 3.0 collective-permute-start.23
  400.6 3.1 collective-permute-done.23
  418.7 5.9 %collective-permute-start.32 = (f32[256,512]{1,0:T(8,128)S(1)}, f32[256,512]{1,0:T(8,128)S(1)}, u32[]{:S(2)}, u32[]{:S(2)}) collective-permute-start(f32[256,512]{1,0:T(8,128)S(1)} %pad_maximum_fusion.1.near1_ref), channel_id=1, source_target_pairs={{0,1},{1,0},{2,3},{3,2},{4,5},{5,4},{6,7},{7,6},{8,9},{9,8},{10,11... | collective-permute-start | bytes 1572872 | tf_op jit(solution)/shard_map/ppermute | solution.py:23
  426.9 3.5 shard_map.59
  (106 shorter events, 57.0 us)
Async XLA Ops:
  4.8 15.1 %collective-permute-start = (s32[40,1024]{1,0:T(8,128)}, s32[40,1024]{1,0:T(8,128)S(1)}, u32[]{:S(2)}, u32[]{:S(2)}) collective-permute-start(s32[40,1024]{1,0:T(8,128)} %get-tuple-element.12), channel_id=1, source_target_pairs={{0,2},{1,3},{2,0},{3,1},{4,6},{5,7},{6,4},{7,5},{8,10},{9,11},{10,... | collective-permute-start | bytes 491528 | tf_op jit(solution)/shard_map/ppermute | solution.py:23
  11.1 221.2 %all-to-all-start = ((f32[128,32,128]{2,1,0:T(8,128)}), f32[128,32,128]{2,1,0:T(8,128)S(1)}, u32[]{:S(2)}, u32[]{:S(2)}) async-start(f32[128,32,128]{2,1,0:T(8,128)} %bitcast.27), calls=%async_computation | async-start | bytes 4194304 | tf_op jit(solution)/shard_map/all_to_all | solution.py:314
  20.5 30.3 %collective-permute-start.1 = (s32[2,40,1024]{2,1,0:T(8,128)S(1)}, s32[2,40,1024]{2,1,0:T(8,128)S(1)}, u32[]{:S(2)}, u32[]{:S(2)}) collective-permute-start(s32[2,40,1024]{2,1,0:T(8,128)S(1)} %pad_add_fusion), channel_id=1, source_target_pairs={{0,4},{1,5},{2,6},{3,7},{4,0},{5,1},{6,2},{7,3},{8,12},{9,13},{10,... | collective-permute-start | bytes 983048 | tf_op jit(solution)/shard_map/ppermute | solution.py:23
  22.9 36.5 %collective-permute-start.3 = (s32[2,40,1024]{2,1,0:T(8,128)S(1)}, s32[2,40,1024]{2,1,0:T(8,128)S(1)}, u32[]{:S(2)}, u32[]{:S(2)}) collective-permute-start(s32[2,40,1024]{2,1,0:T(8,128)S(1)} %pad_add_fusion), channel_id=1, source_target_pairs={{0,12},{1,13},{2,14},{3,15},{4,8},{5,9},{6,10},{7,11},{8,4},{9,5},... | collective-permute-start | bytes 983048 | tf_op jit(solution)/shard_map/ppermute | solution.py:23
  24.7 34.6 %collective-permute-start.2 = (s32[2,40,1024]{2,1,0:T(8,128)S(1)}, s32[2,40,1024]{2,1,0:T(8,128)S(1)}, u32[]{:S(2)}, u32[]{:S(2)}) collective-permute-start(s32[2,40,1024]{2,1,0:T(8,128)S(1)} %pad_add_fusion), channel_id=1, source_target_pairs={{0,8},{1,9},{2,10},{3,11},{4,12},{5,13},{6,14},{7,15},{8,0},{9,1},... | collective-permute-start | bytes 983048 | tf_op jit(solution)/shard_map/ppermute | solution.py:23
  268.3 13.9 %collective-permute-start.8 = (f32[64,512]{1,0:T(8,128)S(1)}, f32[64,512]{1,0:T(8,128)S(1)}, u32[]{:S(2)}, u32[]{:S(2)}) collective-permute-start(f32[64,512]{1,0:T(8,128)S(1)} %get-tuple-element.22), channel_id=1, source_target_pairs={{0,12},{1,13},{2,14},{3,15},{4,8},{5,9},{6,10},{7,11},{8,4},{9,5},... | collective-permute-start | bytes 393224 | tf_op jit(solution)/shard_map/ppermute | solution.py:23
  269.3 12.9 %collective-permute-start.7 = (f32[64,512]{1,0:T(8,128)S(1)}, f32[64,512]{1,0:T(8,128)S(1)}, u32[]{:S(2)}, u32[]{:S(2)}) collective-permute-start(f32[64,512]{1,0:T(8,128)S(1)} %get-tuple-element.23), channel_id=1, source_target_pairs={{0,4},{1,5},{2,6},{3,7},{4,0},{5,1},{6,2},{7,3},{8,12},{9,13},{10,... | collective-permute-start | bytes 393224 | tf_op jit(solution)/shard_map/ppermute | solution.py:23
  269.3 12.9 %collective-permute-start.6 = (f32[64,512]{1,0:T(8,128)S(1)}, f32[64,512]{1,0:T(8,128)S(1)}, u32[]{:S(2)}, u32[]{:S(2)}) collective-permute-start(f32[64,512]{1,0:T(8,128)S(1)} %get-tuple-element.24), channel_id=1, source_target_pairs={{0,8},{1,9},{2,10},{3,11},{4,12},{5,13},{6,14},{7,15},{8,0},{9,1},... | collective-permute-start | bytes 393224 | tf_op jit(solution)/shard_map/ppermute | solution.py:23
  273.5 56.3 %all-to-all-start.1 = ((s32[128,24,128]{2,1,0:T(8,128)}), s32[128,24,128]{2,1,0:T(8,128)S(1)}, u32[]{:S(2)}, u32[]{:S(2)}) async-start(s32[128,24,128]{2,1,0:T(8,128)} %bitcast.11), calls=%async_computation.1 | async-start | bytes 3145728 | tf_op jit(solution)/shard_map/all_to_all | solution.py:314
  282.2 22.4 %collective-permute-start.11 = (f32[64,512]{1,0:T(8,128)S(1)}, f32[64,512]{1,0:T(8,128)S(1)}, u32[]{:S(2)}, u32[]{:S(2)}) collective-permute-start(f32[64,512]{1,0:T(8,128)S(1)} %fusion.1), channel_id=1, source_target_pairs={{0,66},{1,67},{2,64},{3,65},{4,70},{5,71},{6,68},{7,69},{8,74},{9,... | collective-permute-start | bytes 393224 | tf_op jit(solution)/shard_map/ppermute | solution.py:23
  285.0 19.6 %collective-permute-start.10 = (f32[64,512]{1,0:T(8,128)S(1)}, f32[64,512]{1,0:T(8,128)S(1)}, u32[]{:S(2)}, u32[]{:S(2)}) collective-permute-start(f32[64,512]{1,0:T(8,128)S(1)} %fusion.1), channel_id=1, source_target_pairs={{0,64},{1,65},{2,66},{3,67},{4,68},{5,69},{6,70},{7,71},{8,72},{9,... | collective-permute-start | bytes 393224 | tf_op jit(solution)/shard_map/ppermute | solution.py:23
  285.0 22.7 %collective-permute-start.9 = (f32[64,512]{1,0:T(8,128)S(1)}, f32[64,512]{1,0:T(8,128)S(1)}, u32[]{:S(2)}, u32[]{:S(2)}) collective-permute-start(f32[64,512]{1,0:T(8,128)S(1)} %fusion.1), channel_id=1, source_target_pairs={{0,2},{1,3},{2,0},{3,1},{4,6},{5,7},{6,4},{7,5},{8,10},{9,11},{10,... | collective-permute-start | bytes 393224 | tf_op jit(solution)/shard_map/ppermute | solution.py:23
  307.7 6.3 %collective-permute-start.14 = (f32[64,512]{1,0:T(8,128)S(1)}, f32[64,512]{1,0:T(8,128)S(1)}, u32[]{:S(2)}, u32[]{:S(2)}) collective-permute-start(f32[64,512]{1,0:T(8,128)S(1)} %add_add_fusion.3), channel_id=1, source_target_pairs={{0,48},{1,49},{2,50},{3,51},{4,52},{5,53},{6,54},{7,55},{8,56},{9,... | collective-permute-start | bytes 393224 | tf_op jit(solution)/shard_map/ppermute | solution.py:23
  310.9 7.0 %collective-permute-start.12 = (f32[64,512]{1,0:T(8,128)S(1)}, f32[64,512]{1,0:T(8,128)S(1)}, u32[]{:S(2)}, u32[]{:S(2)}) collective-permute-start(f32[64,512]{1,0:T(8,128)S(1)} %add_add_fusion.3), channel_id=1, source_target_pairs={{0,32},{1,33},{2,34},{3,35},{4,36},{5,37},{6,38},{7,39},{8,40},{9,... | collective-permute-start | bytes 393224 | tf_op jit(solution)/shard_map/ppermute | solution.py:23
  318.0 7.9 %collective-permute-start.17 = (f32[64,512]{1,0:T(8,128)S(1)}, f32[64,512]{1,0:T(8,128)S(1)}, u32[]{:S(2)}, u32[]{:S(2)}) collective-permute-start(f32[64,512]{1,0:T(8,128)S(1)} %add_add_fusion.2), channel_id=1, source_target_pairs={{0,12},{1,13},{2,14},{3,15},{4,8},{5,9},{6,10},{7,11},{8,4},{9,5},... | collective-permute-start | bytes 393224 | tf_op jit(solution)/shard_map/ppermute | solution.py:23
  320.8 5.4 %collective-permute-start.16 = (f32[64,512]{1,0:T(8,128)S(1)}, f32[64,512]{1,0:T(8,128)S(1)}, u32[]{:S(2)}, u32[]{:S(2)}) collective-permute-start(f32[64,512]{1,0:T(8,128)S(1)} %add_add_fusion.2), channel_id=1, source_target_pairs={{0,8},{1,9},{2,10},{3,11},{4,12},{5,13},{6,14},{7,15},{8,0},{9,1},... | collective-permute-start | bytes 393224 | tf_op jit(solution)/shard_map/ppermute | solution.py:23
  385.8 6.0 %collective-permute-start.22 = (f32[64,512]{1,0:T(8,128)S(1)}, f32[64,512]{1,0:T(8,128)S(1)}, u32[]{:S(2)}, u32[]{:S(2)}) collective-permute-start(f32[64,512]{1,0:T(8,128)S(1)} %get-tuple-element.19), channel_id=1, source_target_pairs={{0,12},{1,13},{2,14},{3,15},{4,8},{5,9},{6,10},{7,11},{8,4},{9,5},... | collective-permute-start | bytes 393224 | tf_op jit(solution)/shard_map/ppermute | solution.py:23
  387.6 7.9 %collective-permute-start.20 = (f32[64,512]{1,0:T(8,128)S(1)}, f32[64,512]{1,0:T(8,128)S(1)}, u32[]{:S(2)}, u32[]{:S(2)}) collective-permute-start(f32[64,512]{1,0:T(8,128)S(1)} %get-tuple-element.21), channel_id=1, source_target_pairs={{0,8},{1,9},{2,10},{3,11},{4,12},{5,13},{6,14},{7,15},{8,0},{9,1},... | collective-permute-start | bytes 393224 | tf_op jit(solution)/shard_map/ppermute | solution.py:23
  396.4 7.3 %collective-permute-start.23 = (f32[64,512]{1,0:T(8,128)S(1)}, f32[64,512]{1,0:T(8,128)S(1)}, u32[]{:S(2)}, u32[]{:S(2)}) collective-permute-start(f32[64,512]{1,0:T(8,128)S(1)} %fusion), channel_id=1, source_target_pairs={{0,2},{1,3},{2,0},{3,1},{4,6},{5,7},{6,4},{7,5},{8,10},{9,11},{10,... | collective-permute-start | bytes 393224 | tf_op jit(solution)/shard_map/ppermute | solution.py:23
  403.8 5.1 %collective-permute-start.28 = (f32[64,512]{1,0:T(8,128)S(1)}, f32[64,512]{1,0:T(8,128)S(1)}, u32[]{:S(2)}, u32[]{:S(2)}) collective-permute-start(f32[64,512]{1,0:T(8,128)S(1)} %add_add_fusion.1), channel_id=1, source_target_pairs={{0,48},{1,49},{2,50},{3,51},{4,52},{5,53},{6,54},{7,55},{8,56},{9,... | collective-permute-start | bytes 393224 | tf_op jit(solution)/shard_map/ppermute | solution.py:23
  406.1 5.4 %collective-permute-start.26 = (f32[64,512]{1,0:T(8,128)S(1)}, f32[64,512]{1,0:T(8,128)S(1)}, u32[]{:S(2)}, u32[]{:S(2)}) collective-permute-start(f32[64,512]{1,0:T(8,128)S(1)} %add_add_fusion.1), channel_id=1, source_target_pairs={{0,32},{1,33},{2,34},{3,35},{4,36},{5,37},{6,38},{7,39},{8,40},{9,... | collective-permute-start | bytes 393224 | tf_op jit(solution)/shard_map/ppermute | solution.py:23
  413.3 5.3 %collective-permute-start.30 = (f32[64,512]{1,0:T(8,128)S(1)}, f32[64,512]{1,0:T(8,128)S(1)}, u32[]{:S(2)}, u32[]{:S(2)}) collective-permute-start(f32[64,512]{1,0:T(8,128)S(1)} %add_add_fusion), channel_id=1, source_target_pairs={{0,8},{1,9},{2,10},{3,11},{4,12},{5,13},{6,14},{7,15},{8,0},{9,1},... | collective-permute-start | bytes 393224 | tf_op jit(solution)/shard_map/ppermute | solution.py:23
  413.3 5.4 %collective-permute-start.29 = (f32[64,512]{1,0:T(8,128)S(1)}, f32[64,512]{1,0:T(8,128)S(1)}, u32[]{:S(2)}, u32[]{:S(2)}) collective-permute-start(f32[64,512]{1,0:T(8,128)S(1)} %add_add_fusion), channel_id=1, source_target_pairs={{0,4},{1,5},{2,6},{3,7},{4,0},{5,1},{6,2},{7,3},{8,12},{9,13},{10,... | collective-permute-start | bytes 393224 | tf_op jit(solution)/shard_map/ppermute | solution.py:23
  418.7 7.4 %collective-permute-start.32 = (f32[256,512]{1,0:T(8,128)S(1)}, f32[256,512]{1,0:T(8,128)S(1)}, u32[]{:S(2)}, u32[]{:S(2)}) collective-permute-start(f32[256,512]{1,0:T(8,128)S(1)} %pad_maximum_fusion.1.near1_ref), channel_id=1, source_target_pairs={{0,1},{1,0},{2,3},{3,2},{4,5},{5,4},{6,7},{7,6},{8,9},{9,8},{10,11... | collective-permute-start | bytes 1572872 | tf_op jit(solution)/shard_map/ppermute | solution.py:23
  (21 other events, 84.4 us)

commit v2 on v1

v2 whole, which is shorter than its diff:
```python
import jax
import jax.numpy as jnp
from jax import lax
from jax.experimental import pallas as pl
from jax.experimental.pallas import tpu as pltpu
from jax.sharding import PartitionSpec as P

F32 = jnp.float32
BF16 = jnp.bfloat16
I32 = jnp.int32
LEARN_RATE = 0.01
BOTH = ("row", "col")
VMEM_LIMIT = 56 * 1024 * 1024


def partners(dx, dyh, dcore, dyl, dz):
    flip_col = dx * 4 + dyh * 2 + dcore
    flip_row = dyl * 4 + dz
    return [(i, i ^ (flip_row * 16 + flip_col)) for i in range(128)]


def swap(v, dx=0, dyh=0, dcore=0, dyl=0, dz=0):
    return lax.ppermute(v, BOTH, partners(dx, dyh, dcore, dyl, dz))


def lanes(x, index):
    return jnp.take_along_axis(x, index, axis=1, mode="promise_in_bounds")


def iota(shape, dim):
    return lax.broadcasted_iota(I32, shape, dim)


def split(x):
    high = x.astype(BF16)
    low = (x - high.astype(F32)).astype(BF16)
    return high, low


def dot_nt(a, b):
    return lax.dot_general(a, b, (((1,), (1,)), ((), ())), preferred_element_type=F32)


def dot_nn(a, b):
    return lax.dot_general(a, b, (((1,), (0,)), ((), ())), preferred_element_type=F32)


def whole(x):
    return pl.BlockSpec(x.shape, lambda *_: (0,) * x.ndim)


def in_vmem(n):
    return [pl.BlockSpec(memory_space=pltpu.VMEM)] * n


def in_smem():
    return pl.BlockSpec(memory_space=pltpu.SMEM)


def lookup(code, low_table, high_table):
    low = code & 127
    return jnp.where(code >= 128, lanes(high_table, low), lanes(low_table, low))


def part_pairs():
    lane = iota((256, 256), 1)
    return jnp.where(iota((256, 256), 0) == 2 * (lane & 127) + (lane >> 7), 1.0, 0.0).astype(BF16)


def tile_rows(start, tile, parity):
    return pl.ds(start + tile * 16 + parity, 8, stride=2)


def pieces_kernel(tile_ref, codes_ref, piece_ref, own_ref, held_ref):
    lane = iota((8, 128), 1)
    left = lane < 64
    for q in range(8):
        cut = slice(q * 128, q * 128 + 128)
        held_ref[q * 32 : q * 32 + 32, :] = codes_ref[:, cut]
        for t in range(2):
            even = held_ref[tile_rows(q * 32, t, 0), :]
            odd = held_ref[tile_rows(q * 32, t, 1), :]
            own_ref[t * 8 : t * 8 + 8, cut] = even
            own_ref[16 + t * 8 : 24 + t * 8, cut] = odd
            pair = [
                jnp.where(left, even, pltpu.roll(odd, 64, 1)),
                jnp.where(left, pltpu.roll(even, 64, 1), odd),
            ]
            for h in range(2):
                for copy in range(8):
                    piece_ref[copy, 2 * q + h, t * 8 : t * 8 + 8, :] = pair[h]
        books = jnp.where(lane == 0, tile_ref[0, q], tile_ref[1, q])
        for h in range(2):
            for copy in range(8):
                piece_ref[copy, 2 * q + h, 16:24, :] = books
    wide = iota((8, 1024), 1)
    rows = []
    for t in range(2):
        row = jnp.zeros((8, 1024), I32)
        for q in range(8):
            row = jnp.where(wide == q, tile_ref[t, q], row)
        rows.append(row)
    own_ref[32:40, :] = jnp.where(iota((8, 1024), 0) == 0, rows[0], rows[1])


def make_pieces(codes, tile_map):
    return pl.pallas_call(
        pieces_kernel,
        out_shape=[jax.ShapeDtypeStruct((8, 16, 24, 128), I32), jax.ShapeDtypeStruct((40, 1024), I32)],
        in_specs=[in_smem()] + in_vmem(1),
        out_specs=in_vmem(2),
        scratch_shapes=[pltpu.VMEM((256, 128), I32)],
    )(tile_map, codes)


def first_kernel(tile_ref, weights_ref, own_ref, books_ref, error_ref, weight_ref):
    parting = part_pairs()
    for q in range(8):
        parted = dot_nn(weights_ref[:, q * 256 : q * 256 + 256], parting)
        weight_ref[q * 64 : q * 64 + 32, :] = parted[:, 0:128]
        weight_ref[q * 64 + 32 : q * 64 + 64, :] = parted[:, 128:256]
    for q in range(8):
        for t in range(2):
            book = books_ref[tile_ref[t, q]]
            for c in range(2):
                tables = [jnp.broadcast_to(book[c : c + 1, k * 128 : k * 128 + 128], (8, 128)) for k in range(2)]
                for parity in range(2):
                    row = parity * 16 + t * 8
                    code = own_ref[row : row + 8, q * 128 : q * 128 + 128]
                    weight = weight_ref[tile_rows((q * 2 + c) * 32, t, parity), :]
                    error_ref[q * 2 + c, row : row + 8, :] = lookup(code, *tables) - weight


def first(weights, own, tile_map, codebooks):
    return pl.pallas_call(
        first_kernel,
        out_shape=jax.ShapeDtypeStruct((16, 32, 128), F32),
        in_specs=[in_smem()] + in_vmem(3),
        out_specs=in_vmem(1)[0],
        scratch_shapes=[pltpu.VMEM((512, 128), F32)],
    )(tile_map, weights, own, codebooks)


def sort_kernel(piece_ref, packed_ref):
    lane = iota((256, 128), 1)
    key = (piece_ref[:, 0:16, :].reshape(256, 128) * 128 + lane).astype(F32)
    k = 2
    while k <= 128:
        j = k // 2
        while j >= 1:
            lower = (lane & j) == 0
            other = jnp.where(lower, pltpu.roll(key, 128 - j, 1), pltpu.roll(key, j, 1))
            rising = ((lane & k) == 0) == lower
            key = jnp.where(rising, jnp.minimum(key, other), jnp.maximum(key, other))
            j //= 2
        k *= 2
    code = key.astype(I32)
    counts = []
    for half in range(2):
        limit = (half * 128 + lane + 1) * 128
        count = jnp.zeros((256, 128), I32)
        for step in (64, 32, 16, 8, 4, 2, 1, 1):
            below = lanes(code, count + (step - 1)) < limit
            count = jnp.where(below, count + step, count)
        counts.append(count)
    packed_ref[0] = (code & 127) | (counts[0] << 8) | (counts[1] << 16)


def sort_codes(pieces):
    return pl.pallas_call(
        sort_kernel,
        out_shape=jax.ShapeDtypeStruct((8, 256, 128), I32),
        grid=(8,),
        in_specs=[pl.BlockSpec((16, 24, 128), lambda j: (j, 0, 0))],
        out_specs=pl.BlockSpec((1, 256, 128), lambda j: (j, 0, 0)),
        compiler_params=pltpu.CompilerParams(vmem_limit_bytes=VMEM_LIMIT),
    )(pieces)


def step_body(second, col_ref, place_ref, hessian_ref, packed_ref, book_row_ref, refs):
    error_refs, refs = refs[:8], refs[8:]
    if second:
        code_refs, (near_ref, far_ref, book_col_ref), refs = refs[:8], refs[8:11], refs[11:]
    keep_ref, send_ref, eh_ref, el_ref, hh_ref, hl_ref, grad_ref, sums_ref, table_ref = refs
    q = pl.program_id(0)
    place = place_ref[0]
    col = col_ref[0]

    @pl.when(q == 0)
    def _():
        if second:
            chosen = jnp.where((book_col_ref[...] ^ place) == iota((256, 512), 1), 1.0, 0.0).astype(BF16)
            total = jnp.zeros((256, 512), F32)
            for part, ref in ((0, near_ref), (1, far_ref)):
                high, low = split(ref[...])
                here = chosen[:, part * 256 : part * 256 + 256]
                total = total + dot_nn(here, high) + dot_nn(here, low)
            table_ref[...] = total * LEARN_RATE
        for core in range(2):
            for kx in range(4):
                for kyh in range(2):
                    origin = col ^ (kx * 4 + kyh * 2 + core)
                    start = pl.multiple_of(origin * 16, 16)
                    tile_base = core * 128 + (kx * 2 + kyh) * 16

                    def column(b, carry, error_ref=error_refs[core * 4 + kx], kyh=kyh, start=start, tile_base=tile_base, code_index=core * 4 + kx):
                        for parity in range(2):
                            for c in range(2):
                                value = error_ref[kyh, b * 2 + c, parity * 16 : parity * 16 + 16, :]
                                if second:
                                    moves = []
                                    for t in range(2):
                                        code = code_refs[code_index][
                                            kyh, parity * 16 + t * 8 : parity * 16 + t * 8 + 8, pl.ds(pl.multiple_of(b * 128, 128), 128)
                                        ]
                                        tables = [
                                            jnp.broadcast_to(
                                                table_ref[pl.ds(tile_base + t * 8 + b, 1), c * 256 + k * 128 : c * 256 + k * 128 + 128],
                                                (8, 128),
                                            )
                                            for k in range(2)
                                        ]
                                        moves.append(lookup(code, *tables))
                                    value = value - jnp.concatenate(moves, axis=0)
                                high, low = split(value)
                                eh_ref[b, pl.ds(parity * 256 + start, 16), c * 128 : c * 128 + 128] = high
                                el_ref[b, pl.ds(parity * 256 + start, 16), c * 128 : c * 128 + 128] = low
                        return carry

                    lax.fori_loop(0, 8, column, 0, unroll=True)

    for j in range(8):
        for c in range(2):
            high, low = split(hessian_ref[pl.ds(c * 8 + j, 128, stride=16), :])
            hh_ref[c * 128 : c * 128 + 128, j * 128 : j * 128 + 128] = high
            hl_ref[c * 128 : c * 128 + 128, j * 128 : j * 128 + 128] = low
    for part in range(4):
        cut = slice(part * 256, part * 256 + 256)
        more = dot_nn(eh_ref[q], hh_ref[:, cut]) + dot_nn(el_ref[q], hh_ref[:, cut]) + dot_nn(eh_ref[q], hl_ref[:, cut])

        @pl.when(q == 0)
        def _():
            grad_ref[part] = more

        @pl.when(q > 0)
        def _():
            grad_ref[part] += more

    @pl.when(q == 7)
    def _():
        parting = part_pairs()
        running = jnp.where((iota((256, 128), 0) & 127) <= iota((256, 128), 1), 1.0, 0.0).astype(BF16)
        lane = iota((32, 128), 1)
        for j in range(8):
            part, cut = j // 2, slice((j % 2) * 128, (j % 2) * 128 + 128)
            both = jnp.concatenate([grad_ref[part, 0:256, cut], grad_ref[part, 256:512, cut]], axis=1)
            high, low = split(both)
            pairs = dot_nn(high, parting) + dot_nn(low, parting)
            packed = packed_ref[j]
            source = packed & 127
            counts = [(packed >> 8) & 255, packed >> 16]
            for c in range(2):
                ordered = lanes(pairs[:, c * 128 : c * 128 + 128], source)
                prefix = dot_nn(jnp.concatenate(split(ordered), axis=1), running)
                upto = []
                for count in counts:
                    value = jnp.where(count > 0, lanes(prefix, jnp.maximum(count - 1, 0)), 0.0)
                    upto.append(value.reshape(32, 8, 128).sum(axis=1))
                before = [pltpu.roll(v, 1, 1) for v in upto]
                at = c * 256
                sums_ref[j, :, at : at + 128] = 2.0 * (upto[0] - jnp.where(lane == 0, 0.0, before[0]))
                sums_ref[j, :, at + 128 : at + 256] = 2.0 * (upto[1] - jnp.where(lane == 0, before[0], before[1]))
        chosen = jnp.where((iota((512, 256), 0) ^ place) == book_row_ref[...], 1.0, 0.0).astype(BF16)
        high, low = split(sums_ref[...].reshape(256, 512))
        total = dot_nn(chosen, high) + dot_nn(chosen, low)
        keep_ref[...] = total[0:256]
        send_ref[...] = total[256:512]


def step(second, col, place, hessian, packed, book_row, *rest):
    def kernel(col_ref, place_ref, hessian_ref, packed_ref, book_row_ref, *refs):
        step_body(second, col_ref, place_ref, hessian_ref, packed_ref, book_row_ref, refs)

    half = jax.ShapeDtypeStruct((256, 512), F32)
    return pl.pallas_call(
        kernel,
        out_shape=[half, half],
        grid=(8,),
        in_specs=[in_smem(), in_smem(), pl.BlockSpec((2048, 128), lambda q: (q, 0)), whole(packed), whole(book_row)]
        + [whole(x) for x in rest],
        out_specs=[pl.BlockSpec((256, 512), lambda q: (0, 0))] * 2,
        scratch_shapes=[
            pltpu.VMEM((8, 512, 256), BF16),
            pltpu.VMEM((8, 512, 256), BF16),
            pltpu.VMEM((256, 1024), BF16),
            pltpu.VMEM((256, 1024), BF16),
            pltpu.VMEM((4, 512, 256), F32),
            pltpu.VMEM((8, 32, 512), F32),
            pltpu.VMEM((256, 512), F32),
        ],
        compiler_params=pltpu.CompilerParams(vmem_limit_bytes=VMEM_LIMIT),
    )(col, place, hessian, packed, book_row, *rest)


def last_kernel(place_ref, books_ref, near0_ref, far0_ref, near1_ref, far1_ref, out_ref):
    place = place_ref[0]
    for part, (a_ref, b_ref) in enumerate(((near0_ref, near1_ref), (far0_ref, far1_ref))):
        for k in range(4):
            start = pl.multiple_of((part * 256 + k * 64) ^ place, 64)
            for c in range(2):
                cut = (slice(k * 64, k * 64 + 64), slice(c * 256, c * 256 + 256))
                moved = LEARN_RATE * (a_ref[cut] + b_ref[cut])
                out_ref[pl.ds(start, 64), c, :] = books_ref[pl.ds(start, 64), c, :] - moved


def last(place, codebooks, *parts):
    vmem = pl.BlockSpec(memory_space=pltpu.VMEM)
    return pl.pallas_call(
        last_kernel,
        out_shape=jax.ShapeDtypeStruct((512, 2, 256), F32),
        in_specs=[pl.BlockSpec(memory_space=pltpu.SMEM)] + [vmem] * 5,
        out_specs=vmem,
    )(place, codebooks, *parts)


def sum_all(keep, send):
    half = keep + swap(send, dcore=1)
    quarter = [half[k * 64 : k * 64 + 64] for k in range(4)]
    got = [None] + [swap(quarter[k], dx=k) for k in (1, 2, 3)]
    s = (quarter[0] + got[2]) + (got[1] + got[3])
    got = [None] + [swap(s, dyl=k & 1, dyh=k >> 1) for k in (1, 2, 3)]
    s = (s + got[2]) + (got[1] + got[3])
    got = [None] + [swap(s, dz=k) for k in (1, 2, 3)]
    s = (s + got[2]) + (got[1] + got[3])
    near = jnp.concatenate([s] + [swap(s, dx=k) for k in (1, 2, 3)])
    return near, swap(near, dcore=1)


def gather_col(own):
    pair = jnp.stack([own, swap(own, dyh=1)])
    near = [pair] + [swap(pair, dx=k) for k in (1, 2, 3)]
    return near + [swap(v, dcore=1) for v in near]


def per_device(hessian, weights, codes, tile_map, codebooks):
    col = lax.axis_index("col").astype(I32)
    place = ((col & 1) * 256 + (col >> 2) * 64).reshape(1)
    col = col.reshape(1)
    rows = hessian.reshape(16384, 128)
    spread, own = make_pieces(codes, tile_map)
    pieces = lax.all_to_all(spread.reshape(128, 24, 128), BOTH, 0, 0, tiled=True)
    errors = gather_col(first(weights, own, tile_map, codebooks))
    packed = sort_codes(pieces)
    book_row = pieces[:, 16, 0:2].reshape(1, 256)
    keep, send = step(False, col, place, rows, packed, book_row, *errors)

    around = gather_col(own)
    book_col = jnp.concatenate([v[:, 32:34, 0:8] for v in around]).reshape(256, 1)
    near0, far0 = sum_all(keep, send)
    keep, send = step(True, col, place, rows, packed, book_row, *errors, *around, near0, far0, book_col)
    near1, far1 = sum_all(keep, send)
    return last(place, codebooks, near0, far0, near1, far1)


def solution(mesh):
    placed = (P("row", None, "col", None), P("col", "row"), P("col", "row"), P("col", "row"), P())
    return jax.shard_map(per_device, mesh=mesh, in_specs=placed, out_specs=P(), check_vma=False)
```

time: 431 us -> 296 us (0.69)
  Pallas kernels: 257 us -> 116 us
  starting transfers between devices: 67.3 us -> 81.8 us
  local copies, waits for them, and re-layouts: 12.2 us -> 3.89 us
  waiting for transfers between devices: 90.6 us -> 85.6 us
    pallas_call x4 -> x5, Pallas kernels: 253 us -> 113 us  [the longest x2 72.4 us: step(): pl.pallas_call(kernel, out_shape=[half, half], grid=(8,), in_specs=[in_sm...]
    ppermute x33 -> x44, starting transfers between devices: 49.8 us -> 70.3 us  [swap(): return lax.ppermute(v, BOTH, partners(dx, dyh, dcore, dyl, dz))]
    all_to_all x2 -> x1, starting transfers between devices: 17.4 us -> 11.5 us  [per_device(): lax.all_to_all(spread.reshape(128, 24, 128), BOTH, 0, 0, tiled=True)]
    ppermute x33 -> x44, waiting for transfers between devices: 90.6 us -> 85.6 us  [swap(): return lax.ppermute(v, BOTH, partners(dx, dyh, dcore, dyl, dz))]
  transfers between devices with their start and end apart: 35 -> 45, of which waited for: 25 -> 23; matrix products, arithmetic and copies ran while one was open for 2% -> 1% of each run, Pallas kernels for 39% -> 13%
where the time goes in v2:
time: 296 us; the launch traced here: 292 us
  Pallas kernels  116 us (39%)
  waiting for transfers between devices  85.6 us (29%)
  starting transfers between devices  81.8 us (28%)
  local copies, waits for them, and re-layouts  3.89 us (1%)
  other arithmetic  3.55 us (1%)
    ppermute x44, waiting for transfers between devices, swap(): return lax.ppermute(v, BOTH, partners(dx, dyh, dcore, dyl, dz))  85.6 us
    pallas_call x2, Pallas kernels, step(): pl.pallas_call(kernel, out_shape=[half, half], grid=(8,), in_specs=[in_sm...  72.4 us
    ppermute x44, starting transfers between devices, swap(): return lax.ppermute(v, BOTH, partners(dx, dyh, dcore, dyl, dz))  70.3 us
    pallas_call x1, Pallas kernels, sort_codes(): pl.pallas_call(sort_kernel, out_shape=jax.ShapeDtypeStruct((8, 256, 128),...  35.8 us
    all_to_all x1, starting transfers between devices, per_device(): lax.all_to_all(spread.reshape(128, 24, 128), BOTH, 0, 0, tiled=True)  11.5 us
  transfers between devices with their start and end apart: 45, of which 23 were waited for; matrix products, arithmetic and copies ran while one was open for 1% of the time, Pallas kernels for 13%

profile of v2, /device:TPU:1, one launch (start us, length us, event | category | flops | bytes accessed | tf_op | source)
XLA Modules:
  0.0 292.0 jit_solution(9845693836386418023)
XLA Ops:
  2.3 11.5 %all-to-all-start = ((s32[128,24,128]{2,1,0:T(8,128)}), s32[128,24,128]{2,1,0:T(8,128)S(1)}, u32[]{:S(2)}, u32[]{:S(2)}) async-start(s32[128,24,128]{2,1,0:T(8,128)} %bitcast.10), calls=%async_computation | async-start | bytes 3145728 | tf_op jit(solution)/shard_map/all_to_all | solution.py:351
  16.3 2.9 collective-permute-start
  19.2 20.2 %collective-permute-done = f32[16,32,128]{2,1,0:T(8,128)S(1)} collective-permute-done((f32[16,32,128]{2,1,0:T(8,128)}, f32[16,32,128]{2,1,0:T(8,128)S(1)}, u32[]{:S(2)}, u32[]{:S(2)}) %collective-permute-start) | collective-permute-done | bytes 262176 | tf_op jit(solution)/shard_map/ppermute | solution.py:23
  45.5 19.9 %collective-permute-done.3.refs_3_ = f32[2,16,32,128]{3,2,1,0:T(8,128)S(1)} collective-permute-done((f32[2,16,32,128]{3,2,1,0:T(8,128)S(1)}, f32[2,16,32,128]{3,2,1,0:T(8,128)S(1)}, u32[]{:S(2)}, u32[]{:S(2)}) %collective-permute-start.3) | collective-permute-done | bytes 524320 | tf_op jit(solution)/shard_map/ppermute | solution.py:23
  69.4 35.8 %shard_map.56.packed_ref = s32[8,256,128]{2,1,0:T(8,128)} custom-call(s32[128,24,128]{2,1,0:T(8,128)} %copy-done), custom_call_target="tpu_custom_call" | custom-call | tf_op jit(solution)/shard_map/pallas_call | solution.py:170
  105.2 33.1 %shard_map.58 = (f32[256,512]{1,0:T(8,128)}, f32[256,512]{1,0:T(8,128)}) custom-call(s32[1]{0:T(128)} %bitcast.1.col_ref, s32[1]{0:T(128)} %bitcast.place_ref, f32[16384,128]{1,0:T(8,128)} %bitcast.8, s32[8,256,128]{2,1,0:T(8,128)} %shard_map.56.packed_ref, s32[1,256]{1,0:T(1,128)} %reshape_squeeze.3.book_row_ref, f32[2,16,32,128]{3,2,1,0:T(8,128)} %copy-done.1, ...), custom_call_target="tpu_custom_call" | custom-call | tf_op jit(solution)/shard_map/pallas_call | solution.py:285
  138.4 6.8 %collective-permute-done.22 = s32[40,1024]{1,0:T(8,128)S(1)} collective-permute-done((s32[40,1024]{1,0:T(8,128)S(1)}, s32[40,1024]{1,0:T(8,128)S(1)}, u32[]{:S(2)}, u32[]{:S(2)}) %collective-permute-start.22) | collective-permute-done | bytes 163872 | tf_op jit(solution)/shard_map/ppermute | solution.py:23
  149.8 2.8 collective-permute-start.11
  152.5 9.4 %collective-permute-done.23.refs_9_ = s32[2,40,1024]{2,1,0:T(8,128)S(1)} collective-permute-done((s32[2,40,1024]{2,1,0:T(8,128)S(1)}, s32[2,40,1024]{2,1,0:T(8,128)S(1)}, u32[]{:S(2)}, u32[]{:S(2)}) %collective-permute-start.23) | collective-permute-done | bytes 327712 | tf_op jit(solution)/shard_map/ppermute | solution.py:23
  161.9 2.8 collective-permute-start.9
  164.7 4.3 %collective-permute-start.26 = (s32[2,40,1024]{2,1,0:T(8,128)S(1)}, s32[2,40,1024]{2,1,0:T(8,128)S(1)}, u32[]{:S(2)}, u32[]{:S(2)}) collective-permute-start(s32[2,40,1024]{2,1,0:T(8,128)S(1)} %pad_add_fusion.refs_8_), channel_id=1, source_target_pairs={{0,1},{1,0},{2,3},{3,2},{4,5},{5,4},{6,7},{7,6},{8,9},{9,8},{10,11... | collective-permute-start | bytes 983048 | tf_op jit(solution)/shard_map/ppermute | solution.py:23
  170.3 3.1 %collective-permute-start.12 = (f32[64,512]{1,0:T(8,128)S(1)}, f32[64,512]{1,0:T(8,128)S(1)}, u32[]{:S(2)}, u32[]{:S(2)}) collective-permute-start(f32[64,512]{1,0:T(8,128)S(1)} %fusion.1), channel_id=1, source_target_pairs={{0,2},{1,3},{2,0},{3,1},{4,6},{5,7},{6,4},{7,5},{8,10},{9,11},{10,... | collective-permute-start | bytes 393224 | tf_op jit(solution)/shard_map/ppermute | solution.py:23
  174.6 2.7 collective-permute-done.12
  177.3 3.4 %collective-permute-start.17 = (f32[64,512]{1,0:T(8,128)S(1)}, f32[64,512]{1,0:T(8,128)S(1)}, u32[]{:S(2)}, u32[]{:S(2)}) collective-permute-start(f32[64,512]{1,0:T(8,128)S(1)} %add_add_fusion.3), channel_id=1, source_target_pairs={{0,48},{1,49},{2,50},{3,51},{4,52},{5,53},{6,54},{7,55},{8,56},{9,... | collective-permute-start | bytes 393224 | tf_op jit(solution)/shard_map/ppermute | solution.py:23
  183.0 5.1 %collective-permute-start.27 = (s32[2,40,1024]{2,1,0:T(8,128)S(1)}, s32[2,40,1024]{2,1,0:T(8,128)S(1)}, u32[]{:S(2)}, u32[]{:S(2)}) collective-permute-start(s32[2,40,1024]{2,1,0:T(8,128)S(1)} %collective-permute-done.23.refs_9_), channel_id=1, source_target_pairs={{0,1},{1,0},{2,3},{3,2},{4,5},{5,4},{6,7},{7,6},{8,9},{9,8},{10,11... | collective-permute-start | bytes 983048 | tf_op jit(solution)/shard_map/ppermute | solution.py:23
  188.1 3.1 %collective-permute-start.20 = (f32[64,512]{1,0:T(8,128)S(1)}, f32[64,512]{1,0:T(8,128)S(1)}, u32[]{:S(2)}, u32[]{:S(2)}) collective-permute-start(f32[64,512]{1,0:T(8,128)S(1)} %add_add_fusion.2), channel_id=1, source_target_pairs={{0,12},{1,13},{2,14},{3,15},{4,8},{5,9},{6,10},{7,11},{8,4},{9,5},... | collective-permute-start | bytes 393224 | tf_op jit(solution)/shard_map/ppermute | solution.py:23
  191.9 2.6 collective-permute-done.20
  194.6 4.5 %collective-permute-start.28 = (s32[2,40,1024]{2,1,0:T(8,128)S(1)}, s32[2,40,1024]{2,1,0:T(8,128)S(1)}, u32[]{:S(2)}, u32[]{:S(2)}) collective-permute-start(s32[2,40,1024]{2,1,0:T(8,128)S(1)} %collective-permute-done.24.refs_10_), channel_id=1, source_target_pairs={{0,1},{1,0},{2,3},{3,2},{4,5},{5,4},{6,7},{7,6},{8,9},{9,8},{10,11... | collective-permute-start | bytes 983048 | tf_op jit(solution)/shard_map/ppermute | solution.py:23
  199.1 2.6 collective-permute-start.21
  204.1 39.3 %shard_map.59 = (f32[256,512]{1,0:T(8,128)}, f32[256,512]{1,0:T(8,128)}) custom-call(s32[1]{0:T(128)} %bitcast.1.col_ref, s32[1]{0:T(128)} %bitcast.place_ref, f32[16384,128]{1,0:T(8,128)} %bitcast.9, s32[8,256,128]{2,1,0:T(8,128)} %shard_map.56.packed_ref, s32[1,256]{1,0:T(1,128)} %reshape_squeeze.3.book_row_ref, f32[2,16,32,128]{3,2,1,0:T(8,128)} %copy-done.1, ...), custom_call_target="tpu_custom_call" | custom-call | tf_op jit(solution)/shard_map/pallas_call | solution.py:285
  253.1 3.5 %collective-permute-done.31 = f32[64,512]{1,0:T(8,128)S(1)} collective-permute-done((f32[64,512]{1,0:T(8,128)S(1)}, f32[64,512]{1,0:T(8,128)S(1)}, u32[]{:S(2)}, u32[]{:S(2)}) %collective-permute-start.31) | collective-permute-done | bytes 131104 | tf_op jit(solution)/shard_map/ppermute | solution.py:23
  261.8 3.1 %collective-permute-done.34 = f32[64,512]{1,0:T(8,128)S(1)} collective-permute-done((f32[64,512]{1,0:T(8,128)S(1)}, f32[64,512]{1,0:T(8,128)S(1)}, u32[]{:S(2)}, u32[]{:S(2)}) %collective-permute-start.34) | collective-permute-done | bytes 131104 | tf_op jit(solution)/shard_map/ppermute | solution.py:23
  279.8 5.9 %collective-permute-start.43 = (f32[256,512]{1,0:T(8,128)S(1)}, f32[256,512]{1,0:T(8,128)S(1)}, u32[]{:S(2)}, u32[]{:S(2)}) collective-permute-start(f32[256,512]{1,0:T(8,128)S(1)} %pad_maximum_fusion.2.near1_ref), channel_id=1, source_target_pairs={{0,1},{1,0},{2,3},{3,2},{4,5},{5,4},{6,7},{7,6},{8,9},{9,8},{10,11... | collective-permute-start | bytes 1572872 | tf_op jit(solution)/shard_map/ppermute | solution.py:23
  288.0 3.5 %shard_map.60 = f32[512,2,256]{2,1,0:T(2,128)} custom-call(s32[1]{0:T(128)} %bitcast.place_ref, f32[512,2,256]{2,1,0:T(2,128)} %books_ref.3, f32[256,512]{1,0:T(8,128)} %copy-done.2, f32[256,512]{1,0:T(8,128)} %copy-done.5, f32[256,512]{1,0:T(8,128)} %copy-done.6, f32[256,512]{1,0:T(8,128)} %copy-done.9), custom_call_target="tpu_custom_call" | custom-call | tf_op jit(solution)/shard_map/pallas_call | solution.py:318
  (131 shorter events, 59.6 us)
Async XLA Ops:
  2.3 65.9 %all-to-all-start = ((s32[128,24,128]{2,1,0:T(8,128)}), s32[128,24,128]{2,1,0:T(8,128)S(1)}, u32[]{:S(2)}, u32[]{:S(2)}) async-start(s32[128,24,128]{2,1,0:T(8,128)} %bitcast.10), calls=%async_computation | async-start | bytes 3145728 | tf_op jit(solution)/shard_map/all_to_all | solution.py:351
  16.3 23.1 %collective-permute-start = (f32[16,32,128]{2,1,0:T(8,128)}, f32[16,32,128]{2,1,0:T(8,128)S(1)}, u32[]{:S(2)}, u32[]{:S(2)}) collective-permute-start(f32[16,32,128]{2,1,0:T(8,128)} %shard_map.57), channel_id=1, source_target_pairs={{0,2},{1,3},{2,0},{3,1},{4,6},{5,7},{6,4},{7,5},{8,10},{9,11},{10,... | collective-permute-start | bytes 786440 | tf_op jit(solution)/shard_map/ppermute | solution.py:23
  40.4 25.0 %collective-permute-start.3 = (f32[2,16,32,128]{3,2,1,0:T(8,128)S(1)}, f32[2,16,32,128]{3,2,1,0:T(8,128)S(1)}, u32[]{:S(2)}, u32[]{:S(2)}) collective-permute-start(f32[2,16,32,128]{3,2,1,0:T(8,128)S(1)} %pad_maximum_fusion.refs_0_), channel_id=1, source_target_pairs={{0,12},{1,13},{2,14},{3,15},{4,8},{5,9},{6,10},{7,11},{8,4},{9,5},... | collective-permute-start | bytes 1572872 | tf_op jit(solution)/shard_map/ppermute | solution.py:23
  43.0 24.3 %collective-permute-start.2 = (f32[2,16,32,128]{3,2,1,0:T(8,128)S(1)}, f32[2,16,32,128]{3,2,1,0:T(8,128)S(1)}, u32[]{:S(2)}, u32[]{:S(2)}) collective-permute-start(f32[2,16,32,128]{3,2,1,0:T(8,128)S(1)} %pad_maximum_fusion.refs_0_), channel_id=1, source_target_pairs={{0,8},{1,9},{2,10},{3,11},{4,12},{5,13},{6,14},{7,15},{8,0},{9,1},... | collective-permute-start | bytes 1572872 | tf_op jit(solution)/shard_map/ppermute | solution.py:23
  43.6 23.8 %collective-permute-start.1 = (f32[2,16,32,128]{3,2,1,0:T(8,128)S(1)}, f32[2,16,32,128]{3,2,1,0:T(8,128)}, u32[]{:S(2)}, u32[]{:S(2)}) collective-permute-start(f32[2,16,32,128]{3,2,1,0:T(8,128)S(1)} %pad_maximum_fusion.refs_0_), channel_id=1, source_target_pairs={{0,4},{1,5},{2,6},{3,7},{4,0},{5,1},{6,2},{7,3},{8,12},{9,13},{10,... | collective-permute-start | bytes 1572872 | tf_op jit(solution)/shard_map/ppermute | solution.py:23
  43.8 61.4 %collective-permute-start.4 = (f32[2,16,32,128]{3,2,1,0:T(8,128)S(1)}, f32[2,16,32,128]{3,2,1,0:T(8,128)}, u32[]{:S(2)}, u32[]{:S(2)}) collective-permute-start(f32[2,16,32,128]{3,2,1,0:T(8,128)S(1)} %pad_maximum_fusion.refs_0_), channel_id=1, source_target_pairs={{0,1},{1,0},{2,3},{3,2},{4,5},{5,4},{6,7},{7,6},{8,9},{9,8},{10,11... | collective-permute-start | bytes 1572872 | tf_op jit(solution)/shard_map/ppermute | solution.py:23
  65.5 39.7 %collective-permute-start.7 = (f32[2,16,32,128]{3,2,1,0:T(8,128)S(1)}, f32[2,16,32,128]{3,2,1,0:T(8,128)}, u32[]{:S(2)}, u32[]{:S(2)}) collective-permute-start(f32[2,16,32,128]{3,2,1,0:T(8,128)S(1)} %collective-permute-done.3.refs_3_), channel_id=1, source_target_pairs={{0,1},{1,0},{2,3},{3,2},{4,5},{5,4},{6,7},{7,6},{8,9},{9,8},{10,11... | collective-permute-start | bytes 1572872 | tf_op jit(solution)/shard_map/ppermute | solution.py:23
  67.3 37.8 %collective-permute-start.6 = (f32[2,16,32,128]{3,2,1,0:T(8,128)S(1)}, f32[2,16,32,128]{3,2,1,0:T(8,128)}, u32[]{:S(2)}, u32[]{:S(2)}) collective-permute-start(f32[2,16,32,128]{3,2,1,0:T(8,128)S(1)} %collective-permute-done.2.refs_2_), channel_id=1, source_target_pairs={{0,1},{1,0},{2,3},{3,2},{4,5},{5,4},{6,7},{7,6},{8,9},{9,8},{10,11... | collective-permute-start | bytes 1572872 | tf_op jit(solution)/shard_map/ppermute | solution.py:23
  67.4 37.7 %collective-permute-start.5 = (f32[2,16,32,128]{3,2,1,0:T(8,128)}, f32[2,16,32,128]{3,2,1,0:T(8,128)}, u32[]{:S(2)}, u32[]{:S(2)}) collective-permute-start(f32[2,16,32,128]{3,2,1,0:T(8,128)} %collective-permute-done.1.refs_1_), channel_id=1, source_target_pairs={{0,1},{1,0},{2,3},{3,2},{4,5},{5,4},{6,7},{7,6},{8,9},{9,8},{10,11... | collective-permute-start | bytes 1572872 | tf_op jit(solution)/shard_map/ppermute | solution.py:23
  138.3 10.3 %collective-permute-start.8 = (f32[256,512]{1,0:T(8,128)}, f32[256,512]{1,0:T(8,128)S(1)}, u32[]{:S(2)}, u32[]{:S(2)}) collective-permute-start(f32[256,512]{1,0:T(8,128)} %get-tuple-element.14), channel_id=1, source_target_pairs={{0,1},{1,0},{2,3},{3,2},{4,5},{5,4},{6,7},{7,6},{8,9},{9,8},{10,11... | collective-permute-start | bytes 1572872 | tf_op jit(solution)/shard_map/ppermute | solution.py:23
  145.3 19.4 %collective-permute-start.25 = (s32[2,40,1024]{2,1,0:T(8,128)S(1)}, s32[2,40,1024]{2,1,0:T(8,128)S(1)}, u32[]{:S(2)}, u32[]{:S(2)}) collective-permute-start(s32[2,40,1024]{2,1,0:T(8,128)S(1)} %pad_add_fusion.refs_8_), channel_id=1, source_target_pairs={{0,12},{1,13},{2,14},{3,15},{4,8},{5,9},{6,10},{7,11},{8,4},{9,5},... | collective-permute-start | bytes 983048 | tf_op jit(solution)/shard_map/ppermute | solution.py:23
  147.8 22.5 %collective-permute-start.24 = (s32[2,40,1024]{2,1,0:T(8,128)S(1)}, s32[2,40,1024]{2,1,0:T(8,128)S(1)}, u32[]{:S(2)}, u32[]{:S(2)}) collective-permute-start(s32[2,40,1024]{2,1,0:T(8,128)S(1)} %pad_add_fusion.refs_8_), channel_id=1, source_target_pairs={{0,8},{1,9},{2,10},{3,11},{4,12},{5,13},{6,14},{7,15},{8,0},{9,1},... | collective-permute-start | bytes 983048 | tf_op jit(solution)/shard_map/ppermute | solution.py:23
  148.4 13.5 %collective-permute-start.23 = (s32[2,40,1024]{2,1,0:T(8,128)S(1)}, s32[2,40,1024]{2,1,0:T(8,128)S(1)}, u32[]{:S(2)}, u32[]{:S(2)}) collective-permute-start(s32[2,40,1024]{2,1,0:T(8,128)S(1)} %pad_add_fusion.refs_8_), channel_id=1, source_target_pairs={{0,4},{1,5},{2,6},{3,7},{4,0},{5,1},{6,2},{7,3},{8,12},{9,13},{10,... | collective-permute-start | bytes 983048 | tf_op jit(solution)/shard_map/ppermute | solution.py:23
  149.8 19.2 %collective-permute-start.11 = (f32[64,512]{1,0:T(8,128)S(1)}, f32[64,512]{1,0:T(8,128)S(1)}, u32[]{:S(2)}, u32[]{:S(2)}) collective-permute-start(f32[64,512]{1,0:T(8,128)S(1)} %get-tuple-element.20), channel_id=1, source_target_pairs={{0,12},{1,13},{2,14},{3,15},{4,8},{5,9},{6,10},{7,11},{8,4},{9,5},... | collective-permute-start | bytes 393224 | tf_op jit(solution)/shard_map/ppermute | solution.py:23
  152.5 16.5 %collective-permute-start.10 = (f32[64,512]{1,0:T(8,128)S(1)}, f32[64,512]{1,0:T(8,128)S(1)}, u32[]{:S(2)}, u32[]{:S(2)}) collective-permute-start(f32[64,512]{1,0:T(8,128)S(1)} %get-tuple-element.21), channel_id=1, source_target_pairs={{0,4},{1,5},{2,6},{3,7},{4,0},{5,1},{6,2},{7,3},{8,12},{9,13},{10,... | collective-permute-start | bytes 393224 | tf_op jit(solution)/shard_map/ppermute | solution.py:23
  161.9 7.5 %collective-permute-start.9 = (f32[64,512]{1,0:T(8,128)S(1)}, f32[64,512]{1,0:T(8,128)S(1)}, u32[]{:S(2)}, u32[]{:S(2)}) collective-permute-start(f32[64,512]{1,0:T(8,128)S(1)} %get-tuple-element.22), channel_id=1, source_target_pairs={{0,8},{1,9},{2,10},{3,11},{4,12},{5,13},{6,14},{7,15},{8,0},{9,1},... | collective-permute-start | bytes 393224 | tf_op jit(solution)/shard_map/ppermute | solution.py:23
  164.7 26.5 %collective-permute-start.26 = (s32[2,40,1024]{2,1,0:T(8,128)S(1)}, s32[2,40,1024]{2,1,0:T(8,128)S(1)}, u32[]{:S(2)}, u32[]{:S(2)}) collective-permute-start(s32[2,40,1024]{2,1,0:T(8,128)S(1)} %pad_add_fusion.refs_8_), channel_id=1, source_target_pairs={{0,1},{1,0},{2,3},{3,2},{4,5},{5,4},{6,7},{7,6},{8,9},{9,8},{10,11... | collective-permute-start | bytes 983048 | tf_op jit(solution)/shard_map/ppermute | solution.py:23
  169.0 32.8 %collective-permute-start.29 = (s32[2,40,1024]{2,1,0:T(8,128)S(1)}, s32[2,40,1024]{2,1,0:T(8,128)S(1)}, u32[]{:S(2)}, u32[]{:S(2)}) collective-permute-start(s32[2,40,1024]{2,1,0:T(8,128)S(1)} %collective-permute-done.25.refs_11_), channel_id=1, source_target_pairs={{0,1},{1,0},{2,3},{3,2},{4,5},{5,4},{6,7},{7,6},{8,9},{9,8},{10,11... | collective-permute-start | bytes 983048 | tf_op jit(solution)/shard_map/ppermute | solution.py:23
  180.6 7.4 %collective-permute-start.16 = (f32[64,512]{1,0:T(8,128)S(1)}, f32[64,512]{1,0:T(8,128)S(1)}, u32[]{:S(2)}, u32[]{:S(2)}) collective-permute-start(f32[64,512]{1,0:T(8,128)S(1)} %add_add_fusion.3), channel_id=1, source_target_pairs={{0,16},{1,17},{2,18},{3,19},{4,20},{5,21},{6,22},{7,23},{8,24},{9,... | collective-permute-start | bytes 393224 | tf_op jit(solution)/shard_map/ppermute | solution.py:23
  180.6 7.4 %collective-permute-start.15 = (f32[64,512]{1,0:T(8,128)S(1)}, f32[64,512]{1,0:T(8,128)S(1)}, u32[]{:S(2)}, u32[]{:S(2)}) collective-permute-start(f32[64,512]{1,0:T(8,128)S(1)} %add_add_fusion.3), channel_id=1, source_target_pairs={{0,32},{1,33},{2,34},{3,35},{4,36},{5,37},{6,38},{7,39},{8,40},{9,... | collective-permute-start | bytes 393224 | tf_op jit(solution)/shard_map/ppermute | solution.py:23
  183.0 18.7 %collective-permute-start.27 = (s32[2,40,1024]{2,1,0:T(8,128)S(1)}, s32[2,40,1024]{2,1,0:T(8,128)S(1)}, u32[]{:S(2)}, u32[]{:S(2)}) collective-permute-start(s32[2,40,1024]{2,1,0:T(8,128)S(1)} %collective-permute-done.23.refs_9_), channel_id=1, source_target_pairs={{0,1},{1,0},{2,3},{3,2},{4,5},{5,4},{6,7},{7,6},{8,9},{9,8},{10,11... | collective-permute-start | bytes 983048 | tf_op jit(solution)/shard_map/ppermute | solution.py:23
  191.2 7.8 %collective-permute-start.19 = (f32[64,512]{1,0:T(8,128)S(1)}, f32[64,512]{1,0:T(8,128)S(1)}, u32[]{:S(2)}, u32[]{:S(2)}) collective-permute-start(f32[64,512]{1,0:T(8,128)S(1)} %add_add_fusion.2), channel_id=1, source_target_pairs={{0,8},{1,9},{2,10},{3,11},{4,12},{5,13},{6,14},{7,15},{8,0},{9,1},... | collective-permute-start | bytes 393224 | tf_op jit(solution)/shard_map/ppermute | solution.py:23
  191.3 7.8 %collective-permute-start.18 = (f32[64,512]{1,0:T(8,128)S(1)}, f32[64,512]{1,0:T(8,128)S(1)}, u32[]{:S(2)}, u32[]{:S(2)}) collective-permute-start(f32[64,512]{1,0:T(8,128)S(1)} %add_add_fusion.2), channel_id=1, source_target_pairs={{0,4},{1,5},{2,6},{3,7},{4,0},{5,1},{6,2},{7,3},{8,12},{9,13},{10,... | collective-permute-start | bytes 393224 | tf_op jit(solution)/shard_map/ppermute | solution.py:23
  248.7 7.9 %collective-permute-start.31 = (f32[64,512]{1,0:T(8,128)S(1)}, f32[64,512]{1,0:T(8,128)S(1)}, u32[]{:S(2)}, u32[]{:S(2)}) collective-permute-start(f32[64,512]{1,0:T(8,128)S(1)} %get-tuple-element.19), channel_id=1, source_target_pairs={{0,8},{1,9},{2,10},{3,11},{4,12},{5,13},{6,14},{7,15},{8,0},{9,1},... | collective-permute-start | bytes 393224 | tf_op jit(solution)/shard_map/ppermute | solution.py:23
  (38 other events, 455.5 us)

commit v3 on v2

--- a/solution.py
+++ b/solution.py
@@ -11,6 +11,8 @@
 LEARN_RATE = 0.01
 BOTH = ("row", "col")
 VMEM_LIMIT = 56 * 1024 * 1024
+STEP_FLOPS = 18 * 10**9
+SORT_FLOPS = 18 * 10**9
 
 
 def partners(dx, dyh, dcore, dyl, dz):
@@ -141,26 +143,58 @@
     )(tile_map, weights, own, codebooks)
 
 
-def sort_kernel(piece_ref, packed_ref):
-    lane = iota((256, 128), 1)
-    key = (piece_ref[:, 0:16, :].reshape(256, 128) * 128 + lane).astype(F32)
+def spot(position):
+    return ((position & 15) << 3) | (position >> 4)
+
+
+def spot_back(lane):
+    return ((lane & 7) << 4) | (lane >> 3)
+
+
+def sort_block(keys):
+    rows = [keys[v * 8 : v * 8 + 8, :] for v in range(16)]
+    sub = iota((8, 128), 0)
     k = 2
     while k <= 128:
         j = k // 2
         while j >= 1:
-            lower = (lane & j) == 0
-            other = jnp.where(lower, pltpu.roll(key, 128 - j, 1), pltpu.roll(key, j, 1))
-            rising = ((lane & k) == 0) == lower
-            key = jnp.where(rising, jnp.minimum(key, other), jnp.maximum(key, other))
+            if j < 16:
+                for v in range(16):
+                    if v & j:
+                        continue
+                    a, b = rows[v], rows[v | j]
+                    small, large = jnp.minimum(a, b), jnp.maximum(a, b)
+                    if k < 16:
+                        rising = (v & k) == 0
+                        rows[v], rows[v | j] = (small, large) if rising else (large, small)
+                    elif k == 128:
+                        rows[v], rows[v | j] = small, large
+                    else:
+                        up = (sub & (k >> 4)) == 0
+                        rows[v], rows[v | j] = jnp.where(up, small, large), jnp.where(up, large, small)
+            else:
+                step = j >> 4
+                lower = (sub & step) == 0
+                up = lower if k == 128 else ((sub & (k >> 4)) == 0) == lower
+                for v in range(16):
+                    other = jnp.where(lower, pltpu.roll(rows[v], 8 - step, 0), pltpu.roll(rows[v], step, 0))
+                    rows[v] = jnp.where(up, jnp.minimum(rows[v], other), jnp.maximum(rows[v], other))
             j //= 2
         k *= 2
-    code = key.astype(I32)
+    return jnp.concatenate(rows, axis=0)
+
+
+def sort_kernel(piece_ref, packed_ref):
+    lane = iota((256, 128), 1)
+    key = (piece_ref[:, 0:16, :].reshape(256, 128) * 128 + lane).astype(F32)
+    halves = [sort_block(key[h * 128 : h * 128 + 128, :].T).T for h in range(2)]
+    code = jnp.concatenate(halves, axis=0).astype(I32)
     counts = []
     for half in range(2):
         limit = (half * 128 + lane + 1) * 128
         count = jnp.zeros((256, 128), I32)
         for step in (64, 32, 16, 8, 4, 2, 1, 1):
-            below = lanes(code, count + (step - 1)) < limit
+            below = lanes(code, spot(count + (step - 1))) < limit
             count = jnp.where(below, count + step, count)
         counts.append(count)
     packed_ref[0] = (code & 127) | (counts[0] << 8) | (counts[1] << 16)
@@ -174,6 +208,7 @@
         in_specs=[pl.BlockSpec((16, 24, 128), lambda j: (j, 0, 0))],
         out_specs=pl.BlockSpec((1, 256, 128), lambda j: (j, 0, 0)),
         compiler_params=pltpu.CompilerParams(vmem_limit_bytes=VMEM_LIMIT),
+        cost_estimate=pl.CostEstimate(flops=SORT_FLOPS, bytes_accessed=3 * 1024 * 1024, transcendentals=0),
     )(pieces)
 
 
@@ -181,13 +216,17 @@
     error_refs, refs = refs[:8], refs[8:]
     if second:
         code_refs, (near_ref, far_ref, book_col_ref), refs = refs[:8], refs[8:11], refs[11:]
-    keep_ref, send_ref, eh_ref, el_ref, hh_ref, hl_ref, grad_ref, sums_ref, table_ref = refs
-    q = pl.program_id(0)
+    keep_ref, send_ref, left_ref, right_ref, grad_ref, sums_ref, table_ref = refs
+    n = pl.program_id(0)
     place = place_ref[0]
     col = col_ref[0]
-
-    @pl.when(q == 0)
+    slot, before = lax.rem(n, 2), lax.rem(n + 1, 2)
+
+    @pl.when(n == 0)
     def _():
+        left_ref[1] = jnp.zeros((512, 768), BF16)
+        right_ref[1] = jnp.zeros((768, 1024), BF16)
+        grad_ref[...] = jnp.zeros((4, 512, 256), F32)
         if second:
             chosen = jnp.where((book_col_ref[...] ^ place) == iota((256, 512), 1), 1.0, 0.0).astype(BF16)
             total = jnp.zeros((256, 512), F32)
@@ -195,61 +234,56 @@
                 high, low = split(ref[...])
                 here = chosen[:, part * 256 : part * 256 + 256]
                 total = total + dot_nn(here, high) + dot_nn(here, low)
-            table_ref[...] = total * LEARN_RATE
-        for core in range(2):
-            for kx in range(4):
-                for kyh in range(2):
-                    origin = col ^ (kx * 4 + kyh * 2 + core)
-                    start = pl.multiple_of(origin * 16, 16)
-                    tile_base = core * 128 + (kx * 2 + kyh) * 16
-
-                    def column(b, carry, error_ref=error_refs[core * 4 + kx], kyh=kyh, start=start, tile_base=tile_base, code_index=core * 4 + kx):
-                        for parity in range(2):
-                            for c in range(2):
-                                value = error_ref[kyh, b * 2 + c, parity * 16 : parity * 16 + 16, :]
-                                if second:
-                                    moves = []
-                                    for t in range(2):
-                                        code = code_refs[code_index][
-                                            kyh, parity * 16 + t * 8 : parity * 16 + t * 8 + 8, pl.ds(pl.multiple_of(b * 128, 128), 128)
-                                        ]
-                                        tables = [
-                                            jnp.broadcast_to(
-                                                table_ref[pl.ds(tile_base + t * 8 + b, 1), c * 256 + k * 128 : c * 256 + k * 128 + 128],
-                                                (8, 128),
-                                            )
-                                            for k in range(2)
-                                        ]
-                                        moves.append(lookup(code, *tables))
-                                    value = value - jnp.concatenate(moves, axis=0)
-                                high, low = split(value)
-                                eh_ref[b, pl.ds(parity * 256 + start, 16), c * 128 : c * 128 + 128] = high
-                                el_ref[b, pl.ds(parity * 256 + start, 16), c * 128 : c * 128 + 128] = low
-                        return carry
-
-                    lax.fori_loop(0, 8, column, 0, unroll=True)
-
+            table_ref[...] = (total * LEARN_RATE).reshape(8, 32, 512)
+
+    for part in range(4):
+        cut = slice(part * 256, part * 256 + 256)
+        for m in range(2):
+            rows = slice(m * 256, m * 256 + 256)
+            grad_ref[part, rows, :] += dot_nn(left_ref[before, rows, :], right_ref[before, :, cut])
+
+    b = jnp.minimum(n, 7)
+    for core in range(2):
+        for kx in range(4):
+            which = core * 4 + kx
+            for kyh in range(2):
+                origin = col ^ (kx * 4 + kyh * 2 + core)
+                start = pl.multiple_of(origin * 16, 16)
+                base = core * 16 + (kx * 2 + kyh) * 2
+                for c in range(2):
+                    if second:
+                        tables = [
+                            [
+                                jnp.broadcast_to(table_ref[b, base + t : base + t + 1, (c * 2 + k) * 128 : (c * 2 + k) * 128 + 128], (8, 128))
+                                for k in range(2)
+                            ]
+                            for t in range(2)
+                        ]
+                    for parity in range(2):
+                        value = error_refs[which][kyh, c, parity * 16 : parity * 16 + 16, :]
+                        if second:
+                            moves = [
+                                lookup(code_refs[which][kyh, parity * 16 + t * 8 : parity * 16 + t * 8 + 8, :], *tables[t])
+                                for t in range(2)
+                            ]
+                            value = value - jnp.concatenate(moves, axis=0)
+                        high, low = split(value)
+                        rows = pl.ds(parity * 256 + start, 16)
+                        left_ref[slot, rows, c * 128 : c * 128 + 128] = high
+                        left_ref[slot, rows, 256 + c * 128 : 256 + c * 128 + 128] = low
+                        left_ref[slot, rows, 512 + c * 128 : 512 + c * 128 + 128] = high
     for j in range(8):
         for c in range(2):
             high, low = split(hessian_ref[pl.ds(c * 8 + j, 128, stride=16), :])
-            hh_ref[c * 128 : c * 128 + 128, j * 128 : j * 128 + 128] = high
-            hl_ref[c * 128 : c * 128 + 128, j * 128 : j * 128 + 128] = low
-    for part in range(4):
-        cut = slice(part * 256, part * 256 + 256)
-        more = dot_nn(eh_ref[q], hh_ref[:, cut]) + dot_nn(el_ref[q], hh_ref[:, cut]) + dot_nn(eh_ref[q], hl_ref[:, cut])
-
-        @pl.when(q == 0)
-        def _():
-            grad_ref[part] = more
-
-        @pl.when(q > 0)
-        def _():
-            grad_ref[part] += more
-
-    @pl.when(q == 7)
+            cut = slice(j * 128, j * 128 + 128)
+            right_ref[slot, c * 128 : c * 128 + 128, cut] = high
+            right_ref[slot, 256 + c * 128 : 256 + c * 128 + 128, cut] = high
+            right_ref[slot, 512 + c * 128 : 512 + c * 128 + 128, cut] = low
+
+    @pl.when(n == 8)
     def _():
         parting = part_pairs()
-        running = jnp.where((iota((256, 128), 0) & 127) <= iota((256, 128), 1), 1.0, 0.0).astype(BF16)
+        running = jnp.where(spot_back(iota((256, 128), 0) & 127) <= iota((256, 128), 1), 1.0, 0.0).astype(BF16)
         lane = iota((32, 128), 1)
         for j in range(8):
             part, cut = j // 2, slice((j % 2) * 128, (j % 2) * 128 + 128)
@@ -266,10 +300,10 @@
                 for count in counts:
                     value = jnp.where(count > 0, lanes(prefix, jnp.maximum(count - 1, 0)), 0.0)
                     upto.append(value.reshape(32, 8, 128).sum(axis=1))
-                before = [pltpu.roll(v, 1, 1) for v in upto]
+                earlier = [pltpu.roll(v, 1, 1) for v in upto]
                 at = c * 256
-                sums_ref[j, :, at : at + 128] = 2.0 * (upto[0] - jnp.where(lane == 0, 0.0, before[0]))
-                sums_ref[j, :, at + 128 : at + 256] = 2.0 * (upto[1] - jnp.where(lane == 0, before[0], before[1]))
+                sums_ref[j, :, at : at + 128] = 2.0 * (upto[0] - jnp.where(lane == 0, 0.0, earlier[0]))
+                sums_ref[j, :, at + 128 : at + 256] = 2.0 * (upto[1] - jnp.where(lane == 0, earlier[0], earlier[1]))
         chosen = jnp.where((iota((512, 256), 0) ^ place) == book_row_ref[...], 1.0, 0.0).astype(BF16)
         high, low = split(sums_ref[...].reshape(256, 512))
         total = dot_nn(chosen, high) + dot_nn(chosen, low)
@@ -282,23 +316,31 @@
         step_body(second, col_ref, place_ref, hessian_ref, packed_ref, book_row_ref, refs)
 
     half = jax.ShapeDtypeStruct((256, 512), F32)
+    errors = [pl.BlockSpec((2, 2, 32, 128), lambda n: (0, jnp.minimum(n, 7), 0, 0))] * 8
+    codes = [pl.BlockSpec((2, 40, 128), lambda n: (0, 0, jnp.minimum(n, 7)))] * 8
     return pl.pallas_call(
         kernel,
         out_shape=[half, half],
-        grid=(8,),
-        in_specs=[in_smem(), in_smem(), pl.BlockSpec((2048, 128), lambda q: (q, 0)), whole(packed), whole(book_row)]
-        + [whole(x) for x in rest],
-        out_specs=[pl.BlockSpec((256, 512), lambda q: (0, 0))] * 2,
+        grid=(9,),
+        in_specs=[
+            in_smem(),
+            in_smem(),
+            pl.BlockSpec((2048, 128), lambda n: (jnp.minimum(n, 7), 0)),
+            whole(packed),
+            whole(book_row),
+        ]
+        + errors
+        + (codes + [whole(x) for x in rest[16:]] if second else []),
+        out_specs=[pl.BlockSpec((256, 512), lambda n: (0, 0))] * 2,
         scratch_shapes=[
-            pltpu.VMEM((8, 512, 256), BF16),
-            pltpu.VMEM((8, 512, 256), BF16),
-            pltpu.VMEM((256, 1024), BF16),
-            pltpu.VMEM((256, 1024), BF16),
+            pltpu.VMEM((2, 512, 768), BF16),
+            pltpu.VMEM((2, 768, 1024), BF16),
             pltpu.VMEM((4, 512, 256), F32),
             pltpu.VMEM((8, 32, 512), F32),
-            pltpu.VMEM((256, 512), F32),
+            pltpu.VMEM((8, 32, 512), F32),
         ],
         compiler_params=pltpu.CompilerParams(vmem_limit_bytes=VMEM_LIMIT),
+        cost_estimate=pl.CostEstimate(flops=STEP_FLOPS, bytes_accessed=16 * 1024 * 1024, transcendentals=0),
     )(col, place, hessian, packed, book_row, *rest)
 
 
@@ -336,10 +378,20 @@
     return near, swap(near, dcore=1)
 
 
-def gather_col(own):
-    pair = jnp.stack([own, swap(own, dyh=1)])
-    near = [pair] + [swap(pair, dx=k) for k in (1, 2, 3)]
-    return near + [swap(v, dcore=1) for v in near]
+def hold(*values):
+    return lax.optimization_barrier(values)
+
+
+def pair_up(own):
+    return jnp.stack([own, swap(own, dyh=1)])
+
+
+def over_x(pair):
+    return [pair] + [swap(pair, dx=k) for k in (1, 2, 3)]
+
+
+def both_cores(near):
+    return list(near) + [swap(v, dcore=1) for v in near]
 
 
 def per_device(hessian, weights, codes, tile_map, codebooks):
@@ -349,13 +401,16 @@
     rows = hessian.reshape(16384, 128)
     spread, own = make_pieces(codes, tile_map)
     pieces = lax.all_to_all(spread.reshape(128, 24, 128), BOTH, 0, 0, tiled=True)
-    errors = gather_col(first(weights, own, tile_map, codebooks))
+    error_pair, code_pair = pair_up(first(weights, own, tile_map, codebooks)), pair_up(own)
+    pieces, error_pair, code_pair = hold(pieces, error_pair, code_pair)
     packed = sort_codes(pieces)
     book_row = pieces[:, 16, 0:2].reshape(1, 256)
+    packed, book_row, code_pair, *errors = hold(packed, book_row, code_pair, *over_x(error_pair))
+    errors = both_cores(errors)
     keep, send = step(False, col, place, rows, packed, book_row, *errors)
-
-    around = gather_col(own)
-    book_col = jnp.concatenate([v[:, 32:34, 0:8] for v in around]).reshape(256, 1)
+    keep, send, *around = hold(keep, send, *over_x(code_pair))
+    around = both_cores(around)
+    book_col = jnp.concatenate([v[:, 32:34, 0:8] for v in around]).reshape(32, 8).T.reshape(256, 1)
     near0, far0 = sum_all(keep, send)
     keep, send = step(True, col, place, rows, packed, book_row, *errors, *around, near0, far0, book_col)
     near1, far1 = sum_all(keep, send)

time: 296 us -> 219 us (0.74); the launches traced: 292 us -> 218 us
  Pallas kernels: 116 us -> 71.7 us
  waiting for transfers between devices: 85.6 us -> 62.7 us
  starting transfers between devices: 81.8 us -> 75 us
    pallas_call x2, Pallas kernels: 72.4 us -> 47 us  [step(): pl.pallas_call(kernel, out_shape=[half, half], grid=(9,), in_specs=[in_sm...]
    ppermute x44, waiting for transfers between devices: 85.6 us -> 62.7 us  [swap(): return lax.ppermute(v, BOTH, partners(dx, dyh, dcore, dyl, dz))]
    pallas_call x1, Pallas kernels: 35.8 us -> 16.4 us  [sort_codes(): pl.pallas_call(sort_kernel, out_shape=jax.ShapeDtypeStruct((8, 256, 128),...]
    ppermute x44, starting transfers between devices: 70.3 us -> 63.5 us  [swap(): return lax.ppermute(v, BOTH, partners(dx, dyh, dcore, dyl, dz))]
  transfers between devices with their start and end apart: 45 -> 45, of which waited for: 23 -> 24; matrix products, arithmetic and copies ran while one was open for 1% -> 2% of each run, Pallas kernels for 13% -> 19%
where the time goes in v3:
time: 219 us; the launch traced here: 218 us
  starting transfers between devices  75 us (34%)
  Pallas kernels  71.7 us (33%)
  waiting for transfers between devices  62.7 us (29%)
  local copies, waits for them, and re-layouts  5.13 us (2%)
  other arithmetic  3.54 us (2%)
    ppermute x44, starting transfers between devices, swap(): return lax.ppermute(v, BOTH, partners(dx, dyh, dcore, dyl, dz))  63.5 us
    ppermute x44, waiting for transfers between devices, swap(): return lax.ppermute(v, BOTH, partners(dx, dyh, dcore, dyl, dz))  62.7 us
    pallas_call x2, Pallas kernels, step(): pl.pallas_call(kernel, out_shape=[half, half], grid=(9,), in_specs=[in_sm...  47 us
    pallas_call x1, Pallas kernels, sort_codes(): pl.pallas_call(sort_kernel, out_shape=jax.ShapeDtypeStruct((8, 256, 128),...  16.4 us
    all_to_all x1, starting transfers between devices, per_device(): lax.all_to_all(spread.reshape(128, 24, 128), BOTH, 0, 0, tiled=True)  11.5 us
  transfers between devices with their start and end apart: 45, of which 24 were waited for; matrix products, arithmetic and copies ran while one was open for 2% of the time, Pallas kernels for 19%

profile of v3, /device:TPU:1, one launch (start us, length us, event | category | flops | bytes accessed | tf_op | source)
XLA Modules:
  0.0 218.4 jit_solution(3303630770879909940)
XLA Ops:
  2.3 11.5 %all-to-all-start = ((s32[128,24,128]{2,1,0:T(8,128)}), s32[128,24,128]{2,1,0:T(8,128)S(1)}, u32[]{:S(2)}, u32[]{:S(2)}) async-start(s32[128,24,128]{2,1,0:T(8,128)} %bitcast.10), calls=%async_computation | async-start | bytes 3145728 | tf_op jit(solution)/shard_map/all_to_all | solution.py:403
  13.8 3.0 %collective-permute-start.1 = (s32[40,1024]{1,0:T(8,128)S(1)}, s32[40,1024]{1,0:T(8,128)S(1)}, u32[]{:S(2)}, u32[]{:S(2)}) collective-permute-start(s32[40,1024]{1,0:T(8,128)S(1)} %copy-done.3), channel_id=1, source_target_pairs={{0,2},{1,3},{2,0},{3,1},{4,6},{5,7},{6,4},{7,5},{8,10},{9,11},{10,... | collective-permute-start | bytes 491528 | tf_op jit(solution)/shard_map/ppermute | solution.py:25
  16.8 2.5 %shard_map.56 = f32[16,32,128]{2,1,0:T(8,128)} custom-call(s32[2,8]{1,0:T(2,128)} %tile_ref.3, bf16[32,2048]{1,0:T(8,128)(2,1)} %weights_ref.1, s32[40,1024]{1,0:T(8,128)} %get-tuple-element.28.own_ref, f32[512,2,256]{2,1,0:T(2,128)} %books_ref.3), custom_call_target="tpu_custom_call" | custom-call | tf_op jit(solution)/shard_map/pallas_call | solution.py:137
  19.4 17.9 %collective-permute-done.1 = s32[40,1024]{1,0:T(8,128)S(1)} collective-permute-done((s32[40,1024]{1,0:T(8,128)S(1)}, s32[40,1024]{1,0:T(8,128)S(1)}, u32[]{:S(2)}, u32[]{:S(2)}) %collective-permute-start.1) | collective-permute-done | bytes 163872 | tf_op jit(solution)/shard_map/ppermute | solution.py:25
  37.3 5.6 %collective-permute-done = f32[16,32,128]{2,1,0:T(8,128)S(1)} collective-permute-done((f32[16,32,128]{2,1,0:T(8,128)}, f32[16,32,128]{2,1,0:T(8,128)S(1)}, u32[]{:S(2)}, u32[]{:S(2)}) %collective-permute-start) | collective-permute-done | bytes 262176 | tf_op jit(solution)/shard_map/ppermute | solution.py:25
  43.9 2.6 %collective-permute-start.4 = (f32[2,16,32,128]{3,2,1,0:T(8,128)S(1)}, f32[2,16,32,128]{3,2,1,0:T(8,128)S(1)}, u32[]{:S(2)}, u32[]{:S(2)}) collective-permute-start(f32[2,16,32,128]{3,2,1,0:T(8,128)S(1)} %pad_maximum_fusion.refs_0_), channel_id=1, source_target_pairs={{0,12},{1,13},{2,14},{3,15},{4,8},{5,9},{6,10},{7,11},{8,4},{9,5},... | collective-permute-start | bytes 1572872 | tf_op jit(solution)/shard_map/ppermute | solution.py:25
  47.3 16.4 %shard_map.57.packed_ref = s32[8,256,128]{2,1,0:T(8,128)} custom-call(s32[128,24,128]{2,1,0:T(8,128)} %copy-done.2), custom_call_target="tpu_custom_call" | custom-call | flops 17999998976 | bytes 3145728 | tf_op jit(solution)/shard_map/pallas_call | solution.py:204
  65.6 3.3 %collective-permute-done.4.refs_3_ = f32[2,16,32,128]{3,2,1,0:T(8,128)S(1)} collective-permute-done((f32[2,16,32,128]{3,2,1,0:T(8,128)S(1)}, f32[2,16,32,128]{3,2,1,0:T(8,128)S(1)}, u32[]{:S(2)}, u32[]{:S(2)}) %collective-permute-start.4) | collective-permute-done | bytes 524320 | tf_op jit(solution)/shard_map/ppermute | solution.py:25
  72.0 2.5 %collective-permute-start.11 = (s32[2,40,1024]{2,1,0:T(8,128)S(1)}, s32[2,40,1024]{2,1,0:T(8,128)S(1)}, u32[]{:S(2)}, u32[]{:S(2)}) collective-permute-start(s32[2,40,1024]{2,1,0:T(8,128)S(1)} %pad_add_fusion.refs_8_), channel_id=1, source_target_pairs={{0,12},{1,13},{2,14},{3,15},{4,8},{5,9},{6,10},{7,11},{8,4},{9,5},... | collective-permute-start | bytes 983048 | tf_op jit(solution)/shard_map/ppermute | solution.py:25
  77.4 22.2 %shard_map.58 = (f32[256,512]{1,0:T(8,128)}, f32[256,512]{1,0:T(8,128)}) custom-call(s32[1]{0:T(128)} %bitcast.1.col_ref, s32[1]{0:T(128)} %bitcast.place_ref, f32[16384,128]{1,0:T(8,128)} %bitcast.17, s32[8,256,128]{2,1,0:T(8,128)} %shard_map.57.packed_ref, s32[1,256]{1,0:T(1,128)} %reshape_squeeze.3.book_row_ref, f32[2,16,32,128]{3,2,1,0:T(8,128)} %copy-done.7, ...), custom_call_target="tpu_custom_call" | custom-call | flops 17999998976 | bytes 16777216 | tf_op jit(solution)/shard_map/pallas_call | solution.py:321
  104.6 2.6 %collective-permute-start.13 = (f32[64,512]{1,0:T(8,128)S(1)}, f32[64,512]{1,0:T(8,128)S(1)}, u32[]{:S(2)}, u32[]{:S(2)}) collective-permute-start(f32[64,512]{1,0:T(8,128)S(1)} %get-tuple-element.54), channel_id=1, source_target_pairs={{0,8},{1,9},{2,10},{3,11},{4,12},{5,13},{6,14},{7,15},{8,0},{9,1},... | collective-permute-start | bytes 393224 | tf_op jit(solution)/shard_map/ppermute | solution.py:25
  109.3 3.7 %collective-permute-done.13 = f32[64,512]{1,0:T(8,128)S(1)} collective-permute-done((f32[64,512]{1,0:T(8,128)S(1)}, f32[64,512]{1,0:T(8,128)S(1)}, u32[]{:S(2)}, u32[]{:S(2)}) %collective-permute-start.13) | collective-permute-done | bytes 131104 | tf_op jit(solution)/shard_map/ppermute | solution.py:25
  113.9 3.1 %collective-permute-start.16 = (f32[64,512]{1,0:T(8,128)S(1)}, f32[64,512]{1,0:T(8,128)S(1)}, u32[]{:S(2)}, u32[]{:S(2)}) collective-permute-start(f32[64,512]{1,0:T(8,128)S(1)} %fusion.1), channel_id=1, source_target_pairs={{0,2},{1,3},{2,0},{3,1},{4,6},{5,7},{6,4},{7,5},{8,10},{9,11},{10,... | collective-permute-start | bytes 393224 | tf_op jit(solution)/shard_map/ppermute | solution.py:25
  118.1 3.1 %collective-permute-done.16 = f32[64,512]{1,0:T(8,128)S(1)} collective-permute-done((f32[64,512]{1,0:T(8,128)S(1)}, f32[64,512]{1,0:T(8,128)S(1)}, u32[]{:S(2)}, u32[]{:S(2)}) %collective-permute-start.16) | collective-permute-done | bytes 131104 | tf_op jit(solution)/shard_map/ppermute | solution.py:25
  121.2 3.2 %collective-permute-start.21 = (f32[64,512]{1,0:T(8,128)S(1)}, f32[64,512]{1,0:T(8,128)S(1)}, u32[]{:S(2)}, u32[]{:S(2)}) collective-permute-start(f32[64,512]{1,0:T(8,128)S(1)} %add_add_fusion.3), channel_id=1, source_target_pairs={{0,48},{1,49},{2,50},{3,51},{4,52},{5,53},{6,54},{7,55},{8,56},{9,... | collective-permute-start | bytes 393224 | tf_op jit(solution)/shard_map/ppermute | solution.py:25
  126.8 5.1 %collective-permute-start.28 = (s32[2,40,1024]{2,1,0:T(8,128)S(1)}, s32[2,40,1024]{2,1,0:T(8,128)S(1)}, u32[]{:S(2)}, u32[]{:S(2)}) collective-permute-start(s32[2,40,1024]{2,1,0:T(8,128)S(1)} %collective-permute-done.10.refs_10_), channel_id=1, source_target_pairs={{0,1},{1,0},{2,3},{3,2},{4,5},{5,4},{6,7},{7,6},{8,9},{9,8},{10,11... | collective-permute-start | bytes 983048 | tf_op jit(solution)/shard_map/ppermute | solution.py:25
  137.0 3.7 %collective-permute-start.29 = (s32[2,40,1024]{2,1,0:T(8,128)S(1)}, s32[2,40,1024]{2,1,0:T(8,128)S(1)}, u32[]{:S(2)}, u32[]{:S(2)}) collective-permute-start(s32[2,40,1024]{2,1,0:T(8,128)S(1)} %collective-permute-done.11.refs_11_), channel_id=1, source_target_pairs={{0,1},{1,0},{2,3},{3,2},{4,5},{5,4},{6,7},{7,6},{8,9},{9,8},{10,11... | collective-permute-start | bytes 983048 | tf_op jit(solution)/shard_map/ppermute | solution.py:25
  145.6 24.8 %shard_map.59 = (f32[256,512]{1,0:T(8,128)}, f32[256,512]{1,0:T(8,128)}) custom-call(s32[1]{0:T(128)} %bitcast.1.col_ref, s32[1]{0:T(128)} %bitcast.place_ref, f32[16384,128]{1,0:T(8,128)} %bitcast.18, s32[8,256,128]{2,1,0:T(8,128)} %shard_map.57.packed_ref, s32[1,256]{1,0:T(1,128)} %reshape_squeeze.3.book_row_ref, f32[2,16,32,128]{3,2,1,0:T(8,128)} %copy-done.7, ...), custom_call_target="tpu_custom_call" | custom-call | flops 17999998976 | bytes 16777216 | tf_op jit(solution)/shard_map/pallas_call | solution.py:321
  175.1 2.6 %collective-permute-start.31 = (f32[64,512]{1,0:T(8,128)S(1)}, f32[64,512]{1,0:T(8,128)S(1)}, u32[]{:S(2)}, u32[]{:S(2)}) collective-permute-start(f32[64,512]{1,0:T(8,128)S(1)} %get-tuple-element.51), channel_id=1, source_target_pairs={{0,8},{1,9},{2,10},{3,11},{4,12},{5,13},{6,14},{7,15},{8,0},{9,1},... | collective-permute-start | bytes 393224 | tf_op jit(solution)/shard_map/ppermute | solution.py:25
  179.8 3.7 %collective-permute-done.31 = f32[64,512]{1,0:T(8,128)S(1)} collective-permute-done((f32[64,512]{1,0:T(8,128)S(1)}, f32[64,512]{1,0:T(8,128)S(1)}, u32[]{:S(2)}, u32[]{:S(2)}) %collective-permute-start.31) | collective-permute-done | bytes 131104 | tf_op jit(solution)/shard_map/ppermute | solution.py:25
  184.5 2.9 %collective-permute-start.34 = (f32[64,512]{1,0:T(8,128)S(1)}, f32[64,512]{1,0:T(8,128)S(1)}, u32[]{:S(2)}, u32[]{:S(2)}) collective-permute-start(f32[64,512]{1,0:T(8,128)S(1)} %fusion), channel_id=1, source_target_pairs={{0,2},{1,3},{2,0},{3,1},{4,6},{5,7},{6,4},{7,5},{8,10},{9,11},{10,... | collective-permute-start | bytes 393224 | tf_op jit(solution)/shard_map/ppermute | solution.py:25
  188.6 3.1 %collective-permute-done.34 = f32[64,512]{1,0:T(8,128)S(1)} collective-permute-done((f32[64,512]{1,0:T(8,128)S(1)}, f32[64,512]{1,0:T(8,128)S(1)}, u32[]{:S(2)}, u32[]{:S(2)}) %collective-permute-start.34) | collective-permute-done | bytes 131104 | tf_op jit(solution)/shard_map/ppermute | solution.py:25
  206.6 5.9 %collective-permute-start.43 = (f32[256,512]{1,0:T(8,128)S(1)}, f32[256,512]{1,0:T(8,128)S(1)}, u32[]{:S(2)}, u32[]{:S(2)}) collective-permute-start(f32[256,512]{1,0:T(8,128)S(1)} %pad_maximum_fusion.2.near1_ref), channel_id=1, source_target_pairs={{0,1},{1,0},{2,3},{3,2},{4,5},{5,4},{6,7},{7,6},{8,9},{9,8},{10,11... | collective-permute-start | bytes 1572872 | tf_op jit(solution)/shard_map/ppermute | solution.py:25
  214.9 3.5 %shard_map.60 = f32[512,2,256]{2,1,0:T(2,128)} custom-call(s32[1]{0:T(128)} %bitcast.place_ref, f32[512,2,256]{2,1,0:T(2,128)} %books_ref.3, f32[256,512]{1,0:T(8,128)} %copy-done, f32[256,512]{1,0:T(8,128)} %copy-done.5, f32[256,512]{1,0:T(8,128)} %copy-done.1, f32[256,512]{1,0:T(8,128)} %copy-done.6), custom_call_target="tpu_custom_call" | custom-call | tf_op jit(solution)/shard_map/pallas_call | solution.py:360
  (138 shorter events, 59.8 us)
Async XLA Ops:
  2.3 41.7 %all-to-all-start = ((s32[128,24,128]{2,1,0:T(8,128)}), s32[128,24,128]{2,1,0:T(8,128)S(1)}, u32[]{:S(2)}, u32[]{:S(2)}) async-start(s32[128,24,128]{2,1,0:T(8,128)} %bitcast.10), calls=%async_computation | async-start | bytes 3145728 | tf_op jit(solution)/shard_map/all_to_all | solution.py:403
  13.8 23.5 %collective-permute-start.1 = (s32[40,1024]{1,0:T(8,128)S(1)}, s32[40,1024]{1,0:T(8,128)S(1)}, u32[]{:S(2)}, u32[]{:S(2)}) collective-permute-start(s32[40,1024]{1,0:T(8,128)S(1)} %copy-done.3), channel_id=1, source_target_pairs={{0,2},{1,3},{2,0},{3,1},{4,6},{5,7},{6,4},{7,5},{8,10},{9,11},{10,... | collective-permute-start | bytes 491528 | tf_op jit(solution)/shard_map/ppermute | solution.py:25
  19.3 23.6 %collective-permute-start = (f32[16,32,128]{2,1,0:T(8,128)}, f32[16,32,128]{2,1,0:T(8,128)S(1)}, u32[]{:S(2)}, u32[]{:S(2)}) collective-permute-start(f32[16,32,128]{2,1,0:T(8,128)} %shard_map.56), channel_id=1, source_target_pairs={{0,2},{1,3},{2,0},{3,1},{4,6},{5,7},{6,4},{7,5},{8,10},{9,11},{10,... | collective-permute-start | bytes 786440 | tf_op jit(solution)/shard_map/ppermute | solution.py:25
  43.9 25.0 %collective-permute-start.4 = (f32[2,16,32,128]{3,2,1,0:T(8,128)S(1)}, f32[2,16,32,128]{3,2,1,0:T(8,128)S(1)}, u32[]{:S(2)}, u32[]{:S(2)}) collective-permute-start(f32[2,16,32,128]{3,2,1,0:T(8,128)S(1)} %pad_maximum_fusion.refs_0_), channel_id=1, source_target_pairs={{0,12},{1,13},{2,14},{3,15},{4,8},{5,9},{6,10},{7,11},{8,4},{9,5},... | collective-permute-start | bytes 1572872 | tf_op jit(solution)/shard_map/ppermute | solution.py:25
  46.5 22.5 %collective-permute-start.3 = (f32[2,16,32,128]{3,2,1,0:T(8,128)S(1)}, f32[2,16,32,128]{3,2,1,0:T(8,128)S(1)}, u32[]{:S(2)}, u32[]{:S(2)}) collective-permute-start(f32[2,16,32,128]{3,2,1,0:T(8,128)S(1)} %pad_maximum_fusion.refs_0_), channel_id=1, source_target_pairs={{0,8},{1,9},{2,10},{3,11},{4,12},{5,13},{6,14},{7,15},{8,0},{9,1},... | collective-permute-start | bytes 1572872 | tf_op jit(solution)/shard_map/ppermute | solution.py:25
  47.1 22.4 %collective-permute-start.2 = (f32[2,16,32,128]{3,2,1,0:T(8,128)S(1)}, f32[2,16,32,128]{3,2,1,0:T(8,128)}, u32[]{:S(2)}, u32[]{:S(2)}) collective-permute-start(f32[2,16,32,128]{3,2,1,0:T(8,128)S(1)} %pad_maximum_fusion.refs_0_), channel_id=1, source_target_pairs={{0,4},{1,5},{2,6},{3,7},{4,0},{5,1},{6,2},{7,3},{8,12},{9,13},{10,... | collective-permute-start | bytes 1572872 | tf_op jit(solution)/shard_map/ppermute | solution.py:25
  72.0 27.5 %collective-permute-start.11 = (s32[2,40,1024]{2,1,0:T(8,128)S(1)}, s32[2,40,1024]{2,1,0:T(8,128)S(1)}, u32[]{:S(2)}, u32[]{:S(2)}) collective-permute-start(s32[2,40,1024]{2,1,0:T(8,128)S(1)} %pad_add_fusion.refs_8_), channel_id=1, source_target_pairs={{0,12},{1,13},{2,14},{3,15},{4,8},{5,9},{6,10},{7,11},{8,4},{9,5},... | collective-permute-start | bytes 983048 | tf_op jit(solution)/shard_map/ppermute | solution.py:25
  74.5 25.1 %collective-permute-start.10 = (s32[2,40,1024]{2,1,0:T(8,128)S(1)}, s32[2,40,1024]{2,1,0:T(8,128)S(1)}, u32[]{:S(2)}, u32[]{:S(2)}) collective-permute-start(s32[2,40,1024]{2,1,0:T(8,128)S(1)} %pad_add_fusion.refs_8_), channel_id=1, source_target_pairs={{0,8},{1,9},{2,10},{3,11},{4,12},{5,13},{6,14},{7,15},{8,0},{9,1},... | collective-permute-start | bytes 983048 | tf_op jit(solution)/shard_map/ppermute | solution.py:25
  76.6 23.0 %collective-permute-start.9 = (s32[2,40,1024]{2,1,0:T(8,128)S(1)}, s32[2,40,1024]{2,1,0:T(8,128)S(1)}, u32[]{:S(2)}, u32[]{:S(2)}) collective-permute-start(s32[2,40,1024]{2,1,0:T(8,128)S(1)} %pad_add_fusion.refs_8_), channel_id=1, source_target_pairs={{0,4},{1,5},{2,6},{3,7},{4,0},{5,1},{6,2},{7,3},{8,12},{9,13},{10,... | collective-permute-start | bytes 983048 | tf_op jit(solution)/shard_map/ppermute | solution.py:25
  100.4 33.8 %collective-permute-start.26 = (s32[2,40,1024]{2,1,0:T(8,128)S(1)}, s32[2,40,1024]{2,1,0:T(8,128)S(1)}, u32[]{:S(2)}, u32[]{:S(2)}) collective-permute-start(s32[2,40,1024]{2,1,0:T(8,128)S(1)} %pad_add_fusion.refs_8_), channel_id=1, source_target_pairs={{0,1},{1,0},{2,3},{3,2},{4,5},{5,4},{6,7},{7,6},{8,9},{9,8},{10,11... | collective-permute-start | bytes 983048 | tf_op jit(solution)/shard_map/ppermute | solution.py:25
  100.5 42.8 %collective-permute-start.27 = (s32[2,40,1024]{2,1,0:T(8,128)S(1)}, s32[2,40,1024]{2,1,0:T(8,128)S(1)}, u32[]{:S(2)}, u32[]{:S(2)}) collective-permute-start(s32[2,40,1024]{2,1,0:T(8,128)S(1)} %collective-permute-done.9.refs_9_), channel_id=1, source_target_pairs={{0,1},{1,0},{2,3},{3,2},{4,5},{5,4},{6,7},{7,6},{8,9},{9,8},{10,11... | collective-permute-start | bytes 983048 | tf_op jit(solution)/shard_map/ppermute | solution.py:25
  103.3 6.0 %collective-permute-start.15 = (f32[64,512]{1,0:T(8,128)S(1)}, f32[64,512]{1,0:T(8,128)S(1)}, u32[]{:S(2)}, u32[]{:S(2)}) collective-permute-start(f32[64,512]{1,0:T(8,128)S(1)} %get-tuple-element.52), channel_id=1, source_target_pairs={{0,12},{1,13},{2,14},{3,15},{4,8},{5,9},{6,10},{7,11},{8,4},{9,5},... | collective-permute-start | bytes 393224 | tf_op jit(solution)/shard_map/ppermute | solution.py:25
  104.6 8.3 %collective-permute-start.13 = (f32[64,512]{1,0:T(8,128)S(1)}, f32[64,512]{1,0:T(8,128)S(1)}, u32[]{:S(2)}, u32[]{:S(2)}) collective-permute-start(f32[64,512]{1,0:T(8,128)S(1)} %get-tuple-element.54), channel_id=1, source_target_pairs={{0,8},{1,9},{2,10},{3,11},{4,12},{5,13},{6,14},{7,15},{8,0},{9,1},... | collective-permute-start | bytes 393224 | tf_op jit(solution)/shard_map/ppermute | solution.py:25
  113.9 7.3 %collective-permute-start.16 = (f32[64,512]{1,0:T(8,128)S(1)}, f32[64,512]{1,0:T(8,128)S(1)}, u32[]{:S(2)}, u32[]{:S(2)}) collective-permute-start(f32[64,512]{1,0:T(8,128)S(1)} %fusion.1), channel_id=1, source_target_pairs={{0,2},{1,3},{2,0},{3,1},{4,6},{5,7},{6,4},{7,5},{8,10},{9,11},{10,... | collective-permute-start | bytes 393224 | tf_op jit(solution)/shard_map/ppermute | solution.py:25
  124.5 7.4 %collective-permute-start.20 = (f32[64,512]{1,0:T(8,128)S(1)}, f32[64,512]{1,0:T(8,128)S(1)}, u32[]{:S(2)}, u32[]{:S(2)}) collective-permute-start(f32[64,512]{1,0:T(8,128)S(1)} %add_add_fusion.3), channel_id=1, source_target_pairs={{0,16},{1,17},{2,18},{3,19},{4,20},{5,21},{6,22},{7,23},{8,24},{9,... | collective-permute-start | bytes 393224 | tf_op jit(solution)/shard_map/ppermute | solution.py:25
  124.5 7.4 %collective-permute-start.19 = (f32[64,512]{1,0:T(8,128)S(1)}, f32[64,512]{1,0:T(8,128)S(1)}, u32[]{:S(2)}, u32[]{:S(2)}) collective-permute-start(f32[64,512]{1,0:T(8,128)S(1)} %add_add_fusion.3), channel_id=1, source_target_pairs={{0,32},{1,33},{2,34},{3,35},{4,36},{5,37},{6,38},{7,39},{8,40},{9,... | collective-permute-start | bytes 393224 | tf_op jit(solution)/shard_map/ppermute | solution.py:25
  126.8 16.4 %collective-permute-start.28 = (s32[2,40,1024]{2,1,0:T(8,128)S(1)}, s32[2,40,1024]{2,1,0:T(8,128)S(1)}, u32[]{:S(2)}, u32[]{:S(2)}) collective-permute-start(s32[2,40,1024]{2,1,0:T(8,128)S(1)} %collective-permute-done.10.refs_10_), channel_id=1, source_target_pairs={{0,1},{1,0},{2,3},{3,2},{4,5},{5,4},{6,7},{7,6},{8,9},{9,8},{10,11... | collective-permute-start | bytes 983048 | tf_op jit(solution)/shard_map/ppermute | solution.py:25
  133.3 7.4 %collective-permute-start.23 = (f32[64,512]{1,0:T(8,128)S(1)}, f32[64,512]{1,0:T(8,128)S(1)}, u32[]{:S(2)}, u32[]{:S(2)}) collective-permute-start(f32[64,512]{1,0:T(8,128)S(1)} %add_add_fusion.2), channel_id=1, source_target_pairs={{0,8},{1,9},{2,10},{3,11},{4,12},{5,13},{6,14},{7,15},{8,0},{9,1},... | collective-permute-start | bytes 393224 | tf_op jit(solution)/shard_map/ppermute | solution.py:25
  134.2 6.5 %collective-permute-start.22 = (f32[64,512]{1,0:T(8,128)S(1)}, f32[64,512]{1,0:T(8,128)S(1)}, u32[]{:S(2)}, u32[]{:S(2)}) collective-permute-start(f32[64,512]{1,0:T(8,128)S(1)} %add_add_fusion.2), channel_id=1, source_target_pairs={{0,4},{1,5},{2,6},{3,7},{4,0},{5,1},{6,2},{7,3},{8,12},{9,13},{10,... | collective-permute-start | bytes 393224 | tf_op jit(solution)/shard_map/ppermute | solution.py:25
  137.0 6.2 %collective-permute-start.29 = (s32[2,40,1024]{2,1,0:T(8,128)S(1)}, s32[2,40,1024]{2,1,0:T(8,128)S(1)}, u32[]{:S(2)}, u32[]{:S(2)}) collective-permute-start(s32[2,40,1024]{2,1,0:T(8,128)S(1)} %collective-permute-done.11.refs_11_), channel_id=1, source_target_pairs={{0,1},{1,0},{2,3},{3,2},{4,5},{5,4},{6,7},{7,6},{8,9},{9,8},{10,11... | collective-permute-start | bytes 983048 | tf_op jit(solution)/shard_map/ppermute | solution.py:25
  173.8 6.0 %collective-permute-start.33 = (f32[64,512]{1,0:T(8,128)S(1)}, f32[64,512]{1,0:T(8,128)S(1)}, u32[]{:S(2)}, u32[]{:S(2)}) collective-permute-start(f32[64,512]{1,0:T(8,128)S(1)} %get-tuple-element.49), channel_id=1, source_target_pairs={{0,12},{1,13},{2,14},{3,15},{4,8},{5,9},{6,10},{7,11},{8,4},{9,5},... | collective-permute-start | bytes 393224 | tf_op jit(solution)/shard_map/ppermute | solution.py:25
  175.1 8.3 %collective-permute-start.31 = (f32[64,512]{1,0:T(8,128)S(1)}, f32[64,512]{1,0:T(8,128)S(1)}, u32[]{:S(2)}, u32[]{:S(2)}) collective-permute-start(f32[64,512]{1,0:T(8,128)S(1)} %get-tuple-element.51), channel_id=1, source_target_pairs={{0,8},{1,9},{2,10},{3,11},{4,12},{5,13},{6,14},{7,15},{8,0},{9,1},... | collective-permute-start | bytes 393224 | tf_op jit(solution)/shard_map/ppermute | solution.py:25
  184.5 7.1 %collective-permute-start.34 = (f32[64,512]{1,0:T(8,128)S(1)}, f32[64,512]{1,0:T(8,128)S(1)}, u32[]{:S(2)}, u32[]{:S(2)}) collective-permute-start(f32[64,512]{1,0:T(8,128)S(1)} %fusion), channel_id=1, source_target_pairs={{0,2},{1,3},{2,0},{3,1},{4,6},{5,7},{6,4},{7,5},{8,10},{9,11},{10,... | collective-permute-start | bytes 393224 | tf_op jit(solution)/shard_map/ppermute | solution.py:25
  206.6 7.4 %collective-permute-start.43 = (f32[256,512]{1,0:T(8,128)S(1)}, f32[256,512]{1,0:T(8,128)S(1)}, u32[]{:S(2)}, u32[]{:S(2)}) collective-permute-start(f32[256,512]{1,0:T(8,128)S(1)} %pad_maximum_fusion.2.near1_ref), channel_id=1, source_target_pairs={{0,1},{1,0},{2,3},{3,2},{4,5},{5,4},{6,7},{7,6},{8,9},{9,8},{10,11... | collective-permute-start | bytes 1572872 | tf_op jit(solution)/shard_map/ppermute | solution.py:25
  (41 other events, 359.1 us)

commit v4 on v3

--- a/solution.py
+++ b/solution.py
@@ -12,7 +12,8 @@
 BOTH = ("row", "col")
 VMEM_LIMIT = 56 * 1024 * 1024
 STEP_FLOPS = 18 * 10**9
-SORT_FLOPS = 18 * 10**9
+SORT_FLOPS = 5 * 10**9
+SPLIT_FLOPS = 9 * 10**9
 
 
 def partners(dx, dyh, dcore, dyl, dz):
@@ -89,12 +90,10 @@
                 jnp.where(left, pltpu.roll(even, 64, 1), odd),
             ]
             for h in range(2):
-                for copy in range(8):
-                    piece_ref[copy, 2 * q + h, t * 8 : t * 8 + 8, :] = pair[h]
+                piece_ref[2 * q + h, t * 8 : t * 8 + 8, :] = pair[h]
         books = jnp.where(lane == 0, tile_ref[0, q], tile_ref[1, q])
         for h in range(2):
-            for copy in range(8):
-                piece_ref[copy, 2 * q + h, 16:24, :] = books
+            piece_ref[2 * q + h, 16:24, :] = books
     wide = iota((8, 1024), 1)
     rows = []
     for t in range(2):
@@ -108,7 +107,7 @@
 def make_pieces(codes, tile_map):
     return pl.pallas_call(
         pieces_kernel,
-        out_shape=[jax.ShapeDtypeStruct((8, 16, 24, 128), I32), jax.ShapeDtypeStruct((40, 1024), I32)],
+        out_shape=[jax.ShapeDtypeStruct((16, 24, 128), I32), jax.ShapeDtypeStruct((40, 1024), I32)],
         in_specs=[in_smem()] + in_vmem(1),
         out_specs=in_vmem(2),
         scratch_shapes=[pltpu.VMEM((256, 128), I32)],
@@ -186,7 +185,7 @@
 
 def sort_kernel(piece_ref, packed_ref):
     lane = iota((256, 128), 1)
-    key = (piece_ref[:, 0:16, :].reshape(256, 128) * 128 + lane).astype(F32)
+    key = (piece_ref[0, :, 0:16, :].reshape(256, 128) * 128 + lane).astype(F32)
     halves = [sort_block(key[h * 128 : h * 128 + 128, :].T).T for h in range(2)]
     code = jnp.concatenate(halves, axis=0).astype(I32)
     counts = []
@@ -203,30 +202,89 @@
 def sort_codes(pieces):
     return pl.pallas_call(
         sort_kernel,
-        out_shape=jax.ShapeDtypeStruct((8, 256, 128), I32),
-        grid=(8,),
-        in_specs=[pl.BlockSpec((16, 24, 128), lambda j: (j, 0, 0))],
+        out_shape=jax.ShapeDtypeStruct((2, 256, 128), I32),
+        grid=(2,),
+        in_specs=[pl.BlockSpec((1, 16, 24, 128), lambda j: (j, 0, 0, 0))],
         out_specs=pl.BlockSpec((1, 256, 128), lambda j: (j, 0, 0)),
         compiler_params=pltpu.CompilerParams(vmem_limit_bytes=VMEM_LIMIT),
-        cost_estimate=pl.CostEstimate(flops=SORT_FLOPS, bytes_accessed=3 * 1024 * 1024, transcendentals=0),
+        cost_estimate=pl.CostEstimate(flops=SORT_FLOPS, bytes_accessed=1024 * 1024, transcendentals=0),
     )(pieces)
 
 
-def step_body(second, col_ref, place_ref, hessian_ref, packed_ref, book_row_ref, refs):
-    error_refs, refs = refs[:8], refs[8:]
+def split_kernel(hessian_ref, right_ref):
+    for j in range(8):
+        for c in range(2):
+            high, low = split(hessian_ref[pl.ds(c * 8 + j, 128, stride=16), :])
+            cut = slice(j * 128, j * 128 + 128)
+            right_ref[0, c * 128 : c * 128 + 128, cut] = high
+            right_ref[0, 256 + c * 128 : 256 + c * 128 + 128, cut] = high
+            right_ref[0, 512 + c * 128 : 512 + c * 128 + 128, cut] = low
+
+
+def split_hessian(rows):
+    return pl.pallas_call(
+        split_kernel,
+        out_shape=jax.ShapeDtypeStruct((8, 768, 1024), BF16),
+        grid=(8,),
+        in_specs=[pl.BlockSpec((2048, 128), lambda q: (q, 0))],
+        out_specs=pl.BlockSpec((1, 768, 1024), lambda q: (q, 0, 0)),
+        compiler_params=pltpu.CompilerParams(vmem_limit_bytes=VMEM_LIMIT),
+        cost_estimate=pl.CostEstimate(flops=SPLIT_FLOPS, bytes_accessed=20 * 1024 * 1024, transcendentals=0),
+    )(rows)
+
+
+def step_body(second, where_ref, packed_refs, rights, book_row_ref, refs):
+    error_refs, refs = (refs[:8], refs[8:16]), refs[16:]
     if second:
-        code_refs, (near_ref, far_ref, book_col_ref), refs = refs[:8], refs[8:11], refs[11:]
-    keep_ref, send_ref, left_ref, right_ref, grad_ref, sums_ref, table_ref = refs
+        code_refs, refs = (refs[:8], refs[8:16]), refs[16:]
+        (near_ref, far_ref, book_col_ref), refs = refs[:3], refs[3:]
+    keep_ref, send_ref, left0_ref, left1_ref, grad_ref, sums_ref, table_ref = refs
     n = pl.program_id(0)
-    place = place_ref[0]
-    col = col_ref[0]
-    slot, before = lax.rem(n, 2), lax.rem(n + 1, 2)
+    row, col, place = where_ref[0], where_ref[1], where_ref[2]
+
+    def multiply(left_ref, right_ref):
+        for part in range(4):
+            for m in range(2):
+                rows = slice(m * 256, m * 256 + 256)
+                more = dot_nn(left_ref[rows, :], right_ref[0, :, part * 256 : part * 256 + 256])
+                grad_ref[2 * part, rows, :] += more[:, 0:128]
+                grad_ref[2 * part + 1, rows, :] += more[:, 128:256]
+
+    def prepare(half, left_ref):
+        b = jnp.minimum(2 * n + half, 7)
+        for core in range(2):
+            for kx in range(4):
+                which = core * 4 + kx
+                for kyh in range(2):
+                    start = pl.multiple_of((col ^ (kx * 4 + kyh * 2 + core)) * 16, 16)
+                    base = core * 16 + (kx * 2 + kyh) * 2
+                    for c in range(2):
+                        if second:
+                            tables = [
+                                [
+                                    jnp.broadcast_to(table_ref[b, base + t : base + t + 1, (c * 2 + k) * 128 : (c * 2 + k) * 128 + 128], (8, 128))
+                                    for k in range(2)
+                                ]
+                                for t in range(2)
+                            ]
+                        for parity in range(2):
+                            value = error_refs[half][which][kyh, c, parity * 16 : parity * 16 + 16, :]
+                            if second:
+                                moves = [
+                                    lookup(code_refs[half][which][kyh, parity * 16 + t * 8 : parity * 16 + t * 8 + 8, :], *tables[t])
+                                    for t in range(2)
+                                ]
+                                value = value - jnp.concatenate(moves, axis=0)
+                            high, low = split(value)
+                            rows = pl.ds(parity * 256 + start, 16)
+                            left_ref[rows, c * 128 : c * 128 + 128] = high
+                            left_ref[rows, 256 + c * 128 : 256 + c * 128 + 128] = low
+                            left_ref[rows, 512 + c * 128 : 512 + c * 128 + 128] = high
 
     @pl.when(n == 0)
     def _():
-        left_ref[1] = jnp.zeros((512, 768), BF16)
-        right_ref[1] = jnp.zeros((768, 1024), BF16)
-        grad_ref[...] = jnp.zeros((4, 512, 256), F32)
+        left1_ref[...] = jnp.zeros((512, 768), BF16)
+        grad_ref[...] = jnp.zeros((8, 512, 128), F32)
         if second:
             chosen = jnp.where((book_col_ref[...] ^ place) == iota((256, 512), 1), 1.0, 0.0).astype(BF16)
             total = jnp.zeros((256, 512), F32)
@@ -236,74 +294,41 @@
                 total = total + dot_nn(here, high) + dot_nn(here, low)
             table_ref[...] = (total * LEARN_RATE).reshape(8, 32, 512)
 
-    for part in range(4):
-        cut = slice(part * 256, part * 256 + 256)
-        for m in range(2):
-            rows = slice(m * 256, m * 256 + 256)
-            grad_ref[part, rows, :] += dot_nn(left_ref[before, rows, :], right_ref[before, :, cut])
-
-    b = jnp.minimum(n, 7)
-    for core in range(2):
-        for kx in range(4):
-            which = core * 4 + kx
-            for kyh in range(2):
-                origin = col ^ (kx * 4 + kyh * 2 + core)
-                start = pl.multiple_of(origin * 16, 16)
-                base = core * 16 + (kx * 2 + kyh) * 2
-                for c in range(2):
-                    if second:
-                        tables = [
-                            [
-                                jnp.broadcast_to(table_ref[b, base + t : base + t + 1, (c * 2 + k) * 128 : (c * 2 + k) * 128 + 128], (8, 128))
-                                for k in range(2)
-                            ]
-                            for t in range(2)
-                        ]
-                    for parity in range(2):
-                        value = error_refs[which][kyh, c, parity * 16 : parity * 16 + 16, :]
-                        if second:
-                            moves = [
-                                lookup(code_refs[which][kyh, parity * 16 + t * 8 : parity * 16 + t * 8 + 8, :], *tables[t])
-                                for t in range(2)
-                            ]
-                            value = value - jnp.concatenate(moves, axis=0)
-                        high, low = split(value)
-                        rows = pl.ds(parity * 256 + start, 16)
-                        left_ref[slot, rows, c * 128 : c * 128 + 128] = high
-                        left_ref[slot, rows, 256 + c * 128 : 256 + c * 128 + 128] = low
-                        left_ref[slot, rows, 512 + c * 128 : 512 + c * 128 + 128] = high
-    for j in range(8):
-        for c in range(2):
-            high, low = split(hessian_ref[pl.ds(c * 8 + j, 128, stride=16), :])
-            cut = slice(j * 128, j * 128 + 128)
-            right_ref[slot, c * 128 : c * 128 + 128, cut] = high
-            right_ref[slot, 256 + c * 128 : 256 + c * 128 + 128, cut] = high
-            right_ref[slot, 512 + c * 128 : 512 + c * 128 + 128, cut] = low
-
-    @pl.when(n == 8)
+    prepare(0, left0_ref)
+    multiply(left1_ref, rights[0])
+
+    @pl.when(n < 4)
+    def _():
+        prepare(1, left1_ref)
+        multiply(left0_ref, rights[1])
+
+    @pl.when(n == 4)
     def _():
         parting = part_pairs()
         running = jnp.where(spot_back(iota((256, 128), 0) & 127) <= iota((256, 128), 1), 1.0, 0.0).astype(BF16)
         lane = iota((32, 128), 1)
-        for j in range(8):
-            part, cut = j // 2, slice((j % 2) * 128, (j % 2) * 128 + 128)
-            both = jnp.concatenate([grad_ref[part, 0:256, cut], grad_ref[part, 256:512, cut]], axis=1)
-            high, low = split(both)
-            pairs = dot_nn(high, parting) + dot_nn(low, parting)
-            packed = packed_ref[j]
-            source = packed & 127
-            counts = [(packed >> 8) & 255, packed >> 16]
-            for c in range(2):
-                ordered = lanes(pairs[:, c * 128 : c * 128 + 128], source)
-                prefix = dot_nn(jnp.concatenate(split(ordered), axis=1), running)
-                upto = []
-                for count in counts:
-                    value = jnp.where(count > 0, lanes(prefix, jnp.maximum(count - 1, 0)), 0.0)
-                    upto.append(value.reshape(32, 8, 128).sum(axis=1))
-                earlier = [pltpu.roll(v, 1, 1) for v in upto]
-                at = c * 256
-                sums_ref[j, :, at : at + 128] = 2.0 * (upto[0] - jnp.where(lane == 0, 0.0, earlier[0]))
-                sums_ref[j, :, at + 128 : at + 256] = 2.0 * (upto[1] - jnp.where(lane == 0, earlier[0], earlier[1]))
+        for kz in range(4):
+            for dyl in range(2):
+                j = row ^ (dyl * 4 + kz)
+                at = kz * 2 + dyl
+                both = jnp.concatenate([grad_ref[j, 0:256, :], grad_ref[j, 256:512, :]], axis=1)
+                high, low = split(both)
+                pairs = dot_nn(high, parting) + dot_nn(low, parting)
+                packed = packed_refs[kz][dyl]
+                source = packed & 127
+                counts = [(packed >> 8) & 255, packed >> 16]
+                for c in range(2):
+                    ordered = lanes(pairs[:, c * 128 : c * 128 + 128], source)
+                    prefix = dot_nn(jnp.concatenate(split(ordered), axis=1), running)
+                    upto = []
+                    for count in counts:
+                        value = jnp.where(count > 0, lanes(prefix, jnp.maximum(count - 1, 0)), 0.0)
+                        upto.append(value.reshape(32, 8, 128).sum(axis=1))
+                    earlier = [pltpu.roll(v, 1, 1) for v in upto]
+                    low_sums = 2.0 * (upto[0] - jnp.where(lane == 0, 0.0, earlier[0]))
+                    high_sums = 2.0 * (upto[1] - jnp.where(lane == 0, earlier[0], earlier[1]))
+                    sums_ref[at, :, c * 256 : c * 256 + 128] = low_sums
+                    sums_ref[at, :, c * 256 + 128 : c * 256 + 256] = high_sums
         chosen = jnp.where((iota((512, 256), 0) ^ place) == book_row_ref[...], 1.0, 0.0).astype(BF16)
         high, low = split(sums_ref[...].reshape(256, 512))
         total = dot_nn(chosen, high) + dot_nn(chosen, low)
@@ -311,37 +336,42 @@
         send_ref[...] = total[256:512]
 
 
-def step(second, col, place, hessian, packed, book_row, *rest):
-    def kernel(col_ref, place_ref, hessian_ref, packed_ref, book_row_ref, *refs):
-        step_body(second, col_ref, place_ref, hessian_ref, packed_ref, book_row_ref, refs)
-
+def step(second, place, packed, right, book_row, errors, codes, rest):
+    def kernel(where_ref, *refs):
+        step_body(second, where_ref, refs[0:4], refs[4:6], refs[6], refs[7:])
+
+    def tile_column(half):
+        return lambda n: jnp.clip(2 * n + half, 0, 7)
+
+    right_specs, error_specs, code_specs = [], [], []
+    for half in (-1, 0):
+        right_specs.append(pl.BlockSpec((1, 768, 1024), lambda n, f=tile_column(half): (f(n), 0, 0)))
+    for half in (0, 1):
+        error_specs += [pl.BlockSpec((2, 2, 32, 128), lambda n, f=tile_column(half): (0, f(n), 0, 0))] * 8
+        code_specs += [pl.BlockSpec((2, 40, 128), lambda n, f=tile_column(half): (0, 0, f(n)))] * 8
     half = jax.ShapeDtypeStruct((256, 512), F32)
-    errors = [pl.BlockSpec((2, 2, 32, 128), lambda n: (0, jnp.minimum(n, 7), 0, 0))] * 8
-    codes = [pl.BlockSpec((2, 40, 128), lambda n: (0, 0, jnp.minimum(n, 7)))] * 8
     return pl.pallas_call(
         kernel,
         out_shape=[half, half],
-        grid=(9,),
-        in_specs=[
-            in_smem(),
-            in_smem(),
-            pl.BlockSpec((2048, 128), lambda n: (jnp.minimum(n, 7), 0)),
-            whole(packed),
-            whole(book_row),
-        ]
-        + errors
-        + (codes + [whole(x) for x in rest[16:]] if second else []),
+        grid=(5,),
+        in_specs=[in_smem()]
+        + [whole(x) for x in packed]
+        + right_specs
+        + [whole(book_row)]
+        + error_specs
+        + (code_specs if second else [])
+        + [whole(x) for x in rest],
         out_specs=[pl.BlockSpec((256, 512), lambda n: (0, 0))] * 2,
         scratch_shapes=[
-            pltpu.VMEM((2, 512, 768), BF16),
-            pltpu.VMEM((2, 768, 1024), BF16),
-            pltpu.VMEM((4, 512, 256), F32),
+            pltpu.VMEM((512, 768), BF16),
+            pltpu.VMEM((512, 768), BF16),
+            pltpu.VMEM((8, 512, 128), F32),
             pltpu.VMEM((8, 32, 512), F32),
             pltpu.VMEM((8, 32, 512), F32),
         ],
         compiler_params=pltpu.CompilerParams(vmem_limit_bytes=VMEM_LIMIT),
         cost_estimate=pl.CostEstimate(flops=STEP_FLOPS, bytes_accessed=16 * 1024 * 1024, transcendentals=0),
-    )(col, place, hessian, packed, book_row, *rest)
+    )(place, *packed, right, right, book_row, *errors, *errors, *codes, *codes, *rest)
 
 
 def last_kernel(place_ref, books_ref, near0_ref, far0_ref, near1_ref, far1_ref, out_ref):
@@ -395,24 +425,31 @@
 
 
 def per_device(hessian, weights, codes, tile_map, codebooks):
-    col = lax.axis_index("col").astype(I32)
-    place = ((col & 1) * 256 + (col >> 2) * 64).reshape(1)
-    col = col.reshape(1)
-    rows = hessian.reshape(16384, 128)
-    spread, own = make_pieces(codes, tile_map)
-    pieces = lax.all_to_all(spread.reshape(128, 24, 128), BOTH, 0, 0, tiled=True)
-    error_pair, code_pair = pair_up(first(weights, own, tile_map, codebooks)), pair_up(own)
-    pieces, error_pair, code_pair = hold(pieces, error_pair, code_pair)
-    packed = sort_codes(pieces)
-    book_row = pieces[:, 16, 0:2].reshape(1, 256)
-    packed, book_row, code_pair, *errors = hold(packed, book_row, code_pair, *over_x(error_pair))
+    row, col = lax.axis_index("row").astype(I32), lax.axis_index("col").astype(I32)
+    place = (col & 1) * 256 + (col >> 2) * 64
+    where = jnp.stack([row, col, place])
+    place = place.reshape(1)
+    pieces, own = make_pieces(codes, tile_map)
+    pieces = lax.all_to_all(pieces, "col", 0, 0, tiled=True)
+    error_pair = pair_up(first(weights, own, tile_map, codebooks))
+    right = split_hessian(hessian.reshape(16384, 128))
+    pieces, right, error_pair, own = hold(pieces, right, error_pair, own)
+
+    errors = over_x(error_pair)
+    piece_pair = jnp.stack([pieces, swap(pieces, dyl=1)])
+    pieces = [piece_pair] + [swap(piece_pair, dz=k) for k in (1, 2, 3)]
+    code_pair = pair_up(own)
+    packed = [sort_codes(v) for v in pieces]
+    book_row = jnp.concatenate([v[:, :, 16, 0:2] for v in pieces]).reshape(1, 256)
+    held = hold(book_row, code_pair, *packed, *errors)
+    book_row, code_pair, packed, errors = held[0], held[1], held[2:6], held[6:]
     errors = both_cores(errors)
-    keep, send = step(False, col, place, rows, packed, book_row, *errors)
+    keep, send = step(False, where, packed, right, book_row, errors, [], [])
     keep, send, *around = hold(keep, send, *over_x(code_pair))
     around = both_cores(around)
     book_col = jnp.concatenate([v[:, 32:34, 0:8] for v in around]).reshape(32, 8).T.reshape(256, 1)
     near0, far0 = sum_all(keep, send)
-    keep, send = step(True, col, place, rows, packed, book_row, *errors, *around, near0, far0, book_col)
+    keep, send = step(True, where, packed, right, book_row, errors, around, [near0, far0, book_col])
     near1, far1 = sum_all(keep, send)
     return last(place, codebooks, near0, far0, near1, far1)
 

time: 219 us -> 232 us (1.059); the launches traced: 218 us -> 227 us
  Pallas kernels: 71.7 us -> 80.8 us
  starting transfers between devices: 75 us -> 82.2 us
  waiting for transfers between devices: 62.7 us -> 56.7 us
    ppermute x44 -> x48, starting transfers between devices: 63.5 us -> 73.8 us  [swap(): return lax.ppermute(v, BOTH, partners(dx, dyh, dcore, dyl, dz))]
    pallas_call x4 -> x8, Pallas kernels: 65.7 us -> 74.8 us  [the longest x2 40.5 us: step(): pl.pallas_call(kernel, out_shape=[half, half], grid=(5,), in_specs=[in_sm...]
    ppermute x44 -> x48, waiting for transfers between devices: 62.7 us -> 56.7 us  [swap(): return lax.ppermute(v, BOTH, partners(dx, dyh, dcore, dyl, dz))]
    all_to_all x1, starting transfers between devices: 11.5 us -> 8.45 us  [per_device(): pieces = lax.all_to_all(pieces, 'col', 0, 0, tiled=True)]
  transfers between devices with their start and end apart: 45 -> 49, of which waited for: 24 -> 27; matrix products, arithmetic and copies ran while one was open for 2% -> 2% of each run, Pallas kernels for 19% -> 24%
where the time goes in v4:
time: 232 us; the launch traced here: 227 us
  starting transfers between devices  82.2 us (35%)
  Pallas kernels  80.8 us (35%)
  waiting for transfers between devices  56.7 us (24%)
  local copies, waits for them, and re-layouts  3.81 us (2%)
  other arithmetic  3.31 us (1%)
    ppermute x48, starting transfers between devices, swap(): return lax.ppermute(v, BOTH, partners(dx, dyh, dcore, dyl, dz))  73.8 us
    ppermute x48, waiting for transfers between devices, swap(): return lax.ppermute(v, BOTH, partners(dx, dyh, dcore, dyl, dz))  56.7 us
    pallas_call x2, Pallas kernels, step(): pl.pallas_call(kernel, out_shape=[half, half], grid=(5,), in_specs=[in_sm...  40.5 us
    pallas_call x4, Pallas kernels, sort_codes(): pl.pallas_call(sort_kernel, out_shape=jax.ShapeDtypeStruct((2, 256, 128),...  21.2 us
    pallas_call x1, Pallas kernels, split_hessian(): pl.pallas_call(split_kernel, out_shape=jax.ShapeDtypeStruct((8, 768, 1024...  11.3 us
    all_to_all x1, starting transfers between devices, per_device(): pieces = lax.all_to_all(pieces, 'col', 0, 0, tiled=True)  8.45 us
  transfers between devices with their start and end apart: 49, of which 27 were waited for; matrix products, arithmetic and copies ran while one was open for 2% of the time, Pallas kernels for 24%

profile of v4, /device:TPU:1, one launch (start us, length us, event | category | flops | bytes accessed | tf_op | source)
XLA Modules:
  0.0 227.4 jit_solution(16119359784653459644)
XLA Ops:
  1.7 8.4 %all-to-all-start = ((s32[16,24,128]{2,1,0:T(8,128)}), s32[16,24,128]{2,1,0:T(8,128)S(1)}, u32[]{:S(2)}, u32[]{:S(2)}) async-start(s32[16,24,128]{2,1,0:T(8,128)} %get-tuple-element.31), calls=%async_computation | async-start | bytes 393216 | tf_op jit(solution)/shard_map/all_to_all | solution.py:433
  12.7 2.9 %collective-permute-start = (f32[16,32,128]{2,1,0:T(8,128)}, f32[16,32,128]{2,1,0:T(8,128)S(1)}, u32[]{:S(2)}, u32[]{:S(2)}) collective-permute-start(f32[16,32,128]{2,1,0:T(8,128)} %shard_map.57), channel_id=1, source_target_pairs={{0,2},{1,3},{2,0},{3,1},{4,6},{5,7},{6,4},{7,5},{8,10},{9,11},{10,... | collective-permute-start | bytes 786440 | tf_op jit(solution)/shard_map/ppermute | solution.py:26
  15.6 11.3 %shard_map.56.refs_4_.refs_5_ = bf16[8,768,1024]{2,1,0:T(8,128)(2,1)} custom-call(f32[16384,128]{1,0:T(8,128)} %bitcast.30), custom_call_target="tpu_custom_call" | custom-call | flops 8999999488 | bytes 20971520 | tf_op jit(solution)/shard_map/pallas_call | solution.py:225
  27.5 2.6 %collective-permute-start.8 = (f32[2,16,32,128]{3,2,1,0:T(8,128)S(1)}, f32[2,16,32,128]{3,2,1,0:T(8,128)S(1)}, u32[]{:S(2)}, u32[]{:S(2)}) collective-permute-start(f32[2,16,32,128]{3,2,1,0:T(8,128)S(1)} %pad_maximum_fusion.refs_7_.refs_15_), channel_id=1, source_target_pairs={{0,12},{1,13},{2,14},{3,15},{4,8},{5,9},{6,10},{7,11},{8,4},{9,5},... | collective-permute-start | bytes 1572872 | tf_op jit(solution)/shard_map/ppermute | solution.py:26
  30.7 3.0 %collective-permute-done.5 = s32[40,1024]{1,0:T(8,128)S(1)} collective-permute-done((s32[40,1024]{1,0:T(8,128)S(1)}, s32[40,1024]{1,0:T(8,128)S(1)}, u32[]{:S(2)}, u32[]{:S(2)}) %collective-permute-start.5) | collective-permute-done | bytes 163872 | tf_op jit(solution)/shard_map/ppermute | solution.py:26
  35.7 3.8 %collective-permute-start.4 = (s32[2,16,24,128]{3,2,1,0:T(8,128)S(1)}, s32[2,16,24,128]{3,2,1,0:T(8,128)S(1)}, u32[]{:S(2)}, u32[]{:S(2)}) collective-permute-start(s32[2,16,24,128]{3,2,1,0:T(8,128)S(1)} %pad_add_fusion.piece_ref), channel_id=1, source_target_pairs={{0,48},{1,49},{2,50},{3,51},{4,52},{5,53},{6,54},{7,55},{8,56},{9,... | collective-permute-start | bytes 1179656 | tf_op jit(solution)/shard_map/ppermute | solution.py:26
  40.3 5.3 %shard_map.58.refs_0_ = s32[2,256,128]{2,1,0:T(8,128)} custom-call(s32[2,16,24,128]{3,2,1,0:T(8,128)} %copy-done.7), custom_call_target="tpu_custom_call" | custom-call | flops 5000000000 | bytes 1048576 | tf_op jit(solution)/shard_map/pallas_call | solution.py:203
  45.6 10.8 %collective-permute-done.4.piece_ref = s32[2,16,24,128]{3,2,1,0:T(8,128)S(1)} collective-permute-done((s32[2,16,24,128]{3,2,1,0:T(8,128)S(1)}, s32[2,16,24,128]{3,2,1,0:T(8,128)S(1)}, u32[]{:S(2)}, u32[]{:S(2)}) %collective-permute-start.4) | collective-permute-done | bytes 393248 | tf_op jit(solution)/shard_map/ppermute | solution.py:26
  57.9 5.4 %shard_map.61.refs_3_ = s32[2,256,128]{2,1,0:T(8,128)} custom-call(s32[2,16,24,128]{3,2,1,0:T(8,128)} %copy-done.10), custom_call_target="tpu_custom_call" | custom-call | flops 5000000000 | bytes 1048576 | tf_op jit(solution)/shard_map/pallas_call | solution.py:203
  63.2 5.3 %shard_map.60.refs_2_ = s32[2,256,128]{2,1,0:T(8,128)} custom-call(s32[2,16,24,128]{3,2,1,0:T(8,128)} %copy-done.11), custom_call_target="tpu_custom_call" | custom-call | flops 5000000000 | bytes 1048576 | tf_op jit(solution)/shard_map/pallas_call | solution.py:203
  69.4 5.3 %shard_map.59.refs_1_ = s32[2,256,128]{2,1,0:T(8,128)} custom-call(s32[2,16,24,128]{3,2,1,0:T(8,128)} %copy-done.9), custom_call_target="tpu_custom_call" | custom-call | flops 5000000000 | bytes 1048576 | tf_op jit(solution)/shard_map/pallas_call | solution.py:203
  81.5 20.3 %shard_map.62 = (f32[256,512]{1,0:T(8,128)}, f32[256,512]{1,0:T(8,128)}) custom-call(s32[3]{0:T(128)} %pad_add_fusion.3.where_ref, s32[2,256,128]{2,1,0:T(8,128)} %shard_map.58.refs_0_, s32[2,256,128]{2,1,0:T(8,128)} %shard_map.59.refs_1_, s32[2,256,128]{2,1,0:T(8,128)} %shard_map.60.refs_2_, s32[2,256,128]{2,1,0:T(8,128)} %shard_map.61.refs_3_, ...), custom_call_target="tpu_custom_call" | custom-call | flops 17999998976 | bytes 16777216 | tf_op jit(solution)/shard_map/pallas_call | solution.py:353
  112.3 3.4 %collective-permute-done.17 = f32[64,512]{1,0:T(8,128)S(1)} collective-permute-done((f32[64,512]{1,0:T(8,128)S(1)}, f32[64,512]{1,0:T(8,128)S(1)}, u32[]{:S(2)}, u32[]{:S(2)}) %collective-permute-start.17) | collective-permute-done | bytes 131104 | tf_op jit(solution)/shard_map/ppermute | solution.py:26
  115.8 2.7 %collective-permute-start.22 = (f32[64,512]{1,0:T(8,128)S(1)}, f32[64,512]{1,0:T(8,128)S(1)}, u32[]{:S(2)}, u32[]{:S(2)}) collective-permute-start(f32[64,512]{1,0:T(8,128)S(1)} %fusion.1), channel_id=1, source_target_pairs={{0,66},{1,67},{2,64},{3,65},{4,70},{5,71},{6,68},{7,69},{8,74},{9,... | collective-permute-start | bytes 393224 | tf_op jit(solution)/shard_map/ppermute | solution.py:26
  122.6 2.8 %collective-permute-done.20 = f32[64,512]{1,0:T(8,128)S(1)} collective-permute-done((f32[64,512]{1,0:T(8,128)S(1)}, f32[64,512]{1,0:T(8,128)S(1)}, u32[]{:S(2)}, u32[]{:S(2)}) %collective-permute-start.20) | collective-permute-done | bytes 131104 | tf_op jit(solution)/shard_map/ppermute | solution.py:26
  125.4 2.8 %collective-permute-start.25 = (f32[64,512]{1,0:T(8,128)S(1)}, f32[64,512]{1,0:T(8,128)S(1)}, u32[]{:S(2)}, u32[]{:S(2)}) collective-permute-start(f32[64,512]{1,0:T(8,128)S(1)} %add_add_fusion.3), channel_id=1, source_target_pairs={{0,48},{1,49},{2,50},{3,51},{4,52},{5,53},{6,54},{7,55},{8,56},{9,... | collective-permute-start | bytes 393224 | tf_op jit(solution)/shard_map/ppermute | solution.py:26
  130.6 14.7 %collective-permute-start.32 = (s32[2,40,1024]{2,1,0:T(8,128)S(1)}, s32[2,40,1024]{2,1,0:T(8,128)S(1)}, u32[]{:S(2)}, u32[]{:S(2)}) collective-permute-start(s32[2,40,1024]{2,1,0:T(8,128)S(1)} %collective-permute-done.14.refs_25_.refs_33_), channel_id=1, source_target_pairs={{0,1},{1,0},{2,3},{3,2},{4,5},{5,4},{6,7},{7,6},{8,9},{9,8},{10,11... | collective-permute-start | bytes 983048 | tf_op jit(solution)/shard_map/ppermute | solution.py:26
  148.7 5.4 %collective-permute-done.28 = f32[64,512]{1,0:T(8,128)S(1)} collective-permute-done((f32[64,512]{1,0:T(8,128)S(1)}, f32[64,512]{1,0:T(8,128)S(1)}, u32[]{:S(2)}, u32[]{:S(2)}) %collective-permute-start.28) | collective-permute-done | bytes 131104 | tf_op jit(solution)/shard_map/ppermute | solution.py:26
  158.5 20.3 %shard_map.63 = (f32[256,512]{1,0:T(8,128)}, f32[256,512]{1,0:T(8,128)}) custom-call(s32[3]{0:T(128)} %pad_add_fusion.3.where_ref, s32[2,256,128]{2,1,0:T(8,128)} %shard_map.58.refs_0_, s32[2,256,128]{2,1,0:T(8,128)} %shard_map.59.refs_1_, s32[2,256,128]{2,1,0:T(8,128)} %shard_map.60.refs_2_, s32[2,256,128]{2,1,0:T(8,128)} %shard_map.61.refs_3_, ...), custom_call_target="tpu_custom_call" | custom-call | flops 17999998976 | bytes 16777216 | tf_op jit(solution)/shard_map/pallas_call | solution.py:353
  188.4 3.4 %collective-permute-done.35 = f32[64,512]{1,0:T(8,128)S(1)} collective-permute-done((f32[64,512]{1,0:T(8,128)S(1)}, f32[64,512]{1,0:T(8,128)S(1)}, u32[]{:S(2)}, u32[]{:S(2)}) %collective-permute-start.35) | collective-permute-done | bytes 131104 | tf_op jit(solution)/shard_map/ppermute | solution.py:26
  197.2 2.8 %collective-permute-done.38 = f32[64,512]{1,0:T(8,128)S(1)} collective-permute-done((f32[64,512]{1,0:T(8,128)S(1)}, f32[64,512]{1,0:T(8,128)S(1)}, u32[]{:S(2)}, u32[]{:S(2)}) %collective-permute-start.38) | collective-permute-done | bytes 131104 | tf_op jit(solution)/shard_map/ppermute | solution.py:26
  200.1 2.7 %collective-permute-start.43 = (f32[64,512]{1,0:T(8,128)S(1)}, f32[64,512]{1,0:T(8,128)S(1)}, u32[]{:S(2)}, u32[]{:S(2)}) collective-permute-start(f32[64,512]{1,0:T(8,128)S(1)} %add_add_fusion.1), channel_id=1, source_target_pairs={{0,48},{1,49},{2,50},{3,51},{4,52},{5,53},{6,54},{7,55},{8,56},{9,... | collective-permute-start | bytes 393224 | tf_op jit(solution)/shard_map/ppermute | solution.py:26
  215.4 5.9 %collective-permute-start.47 = (f32[256,512]{1,0:T(8,128)S(1)}, f32[256,512]{1,0:T(8,128)S(1)}, u32[]{:S(2)}, u32[]{:S(2)}) collective-permute-start(f32[256,512]{1,0:T(8,128)S(1)} %pad_maximum_fusion.2.near1_ref), channel_id=1, source_target_pairs={{0,1},{1,0},{2,3},{3,2},{4,5},{5,4},{6,7},{7,6},{8,9},{9,8},{10,11... | collective-permute-start | bytes 1572872 | tf_op jit(solution)/shard_map/ppermute | solution.py:26
  223.6 3.5 %shard_map.64 = f32[512,2,256]{2,1,0:T(2,128)} custom-call(s32[1]{0:T(128)} %bitcast.place_ref, f32[512,2,256]{2,1,0:T(2,128)} %books_ref.3, f32[256,512]{1,0:T(8,128)} %copy-done, f32[256,512]{1,0:T(8,128)} %copy-done.4, f32[256,512]{1,0:T(8,128)} %copy-done.1, f32[256,512]{1,0:T(8,128)} %copy-done.5), custom_call_target="tpu_custom_call" | custom-call | tf_op jit(solution)/shard_map/pallas_call | solution.py:390
  (163 shorter events, 72.2 us)
Async XLA Ops:
  1.7 25.2 %all-to-all-start = ((s32[16,24,128]{2,1,0:T(8,128)}), s32[16,24,128]{2,1,0:T(8,128)S(1)}, u32[]{:S(2)}, u32[]{:S(2)}) async-start(s32[16,24,128]{2,1,0:T(8,128)} %get-tuple-element.31), calls=%async_computation | async-start | bytes 393216 | tf_op jit(solution)/shard_map/all_to_all | solution.py:433
  12.7 14.2 %collective-permute-start = (f32[16,32,128]{2,1,0:T(8,128)}, f32[16,32,128]{2,1,0:T(8,128)S(1)}, u32[]{:S(2)}, u32[]{:S(2)}) collective-permute-start(f32[16,32,128]{2,1,0:T(8,128)} %shard_map.57), channel_id=1, source_target_pairs={{0,2},{1,3},{2,0},{3,1},{4,6},{5,7},{6,4},{7,5},{8,10},{9,11},{10,... | collective-permute-start | bytes 786440 | tf_op jit(solution)/shard_map/ppermute | solution.py:26
  26.9 6.7 %collective-permute-start.5 = (s32[40,1024]{1,0:T(8,128)S(1)}, s32[40,1024]{1,0:T(8,128)S(1)}, u32[]{:S(2)}, u32[]{:S(2)}) collective-permute-start(s32[40,1024]{1,0:T(8,128)S(1)} %copy-done.3), channel_id=1, source_target_pairs={{0,2},{1,3},{2,0},{3,1},{4,6},{5,7},{6,4},{7,5},{8,10},{9,11},{10,... | collective-permute-start | bytes 491528 | tf_op jit(solution)/shard_map/ppermute | solution.py:26
  27.1 8.6 %collective-permute-start.1 = (s32[16,24,128]{2,1,0:T(8,128)S(1)}, s32[16,24,128]{2,1,0:T(8,128)S(1)}, u32[]{:S(2)}, u32[]{:S(2)}) collective-permute-start(s32[16,24,128]{2,1,0:T(8,128)S(1)} %all-to-all-done), channel_id=1, source_target_pairs={{0,64},{1,65},{2,66},{3,67},{4,68},{5,69},{6,70},{7,71},{8,72},{9,... | collective-permute-start | bytes 589832 | tf_op jit(solution)/shard_map/ppermute | solution.py:26
  27.5 47.1 %collective-permute-start.8 = (f32[2,16,32,128]{3,2,1,0:T(8,128)S(1)}, f32[2,16,32,128]{3,2,1,0:T(8,128)S(1)}, u32[]{:S(2)}, u32[]{:S(2)}) collective-permute-start(f32[2,16,32,128]{3,2,1,0:T(8,128)S(1)} %pad_maximum_fusion.refs_7_.refs_15_), channel_id=1, source_target_pairs={{0,12},{1,13},{2,14},{3,15},{4,8},{5,9},{6,10},{7,11},{8,4},{9,5},... | collective-permute-start | bytes 1572872 | tf_op jit(solution)/shard_map/ppermute | solution.py:26
  30.1 44.5 %collective-permute-start.7 = (f32[2,16,32,128]{3,2,1,0:T(8,128)S(1)}, f32[2,16,32,128]{3,2,1,0:T(8,128)}, u32[]{:S(2)}, u32[]{:S(2)}) collective-permute-start(f32[2,16,32,128]{3,2,1,0:T(8,128)S(1)} %pad_maximum_fusion.refs_7_.refs_15_), channel_id=1, source_target_pairs={{0,8},{1,9},{2,10},{3,11},{4,12},{5,13},{6,14},{7,15},{8,0},{9,1},... | collective-permute-start | bytes 1572872 | tf_op jit(solution)/shard_map/ppermute | solution.py:26
  35.7 20.6 %collective-permute-start.4 = (s32[2,16,24,128]{3,2,1,0:T(8,128)S(1)}, s32[2,16,24,128]{3,2,1,0:T(8,128)S(1)}, u32[]{:S(2)}, u32[]{:S(2)}) collective-permute-start(s32[2,16,24,128]{3,2,1,0:T(8,128)S(1)} %pad_add_fusion.piece_ref), channel_id=1, source_target_pairs={{0,48},{1,49},{2,50},{3,51},{4,52},{5,53},{6,54},{7,55},{8,56},{9,... | collective-permute-start | bytes 1179656 | tf_op jit(solution)/shard_map/ppermute | solution.py:26
  39.6 18.1 %collective-permute-start.3 = (s32[2,16,24,128]{3,2,1,0:T(8,128)S(1)}, s32[2,16,24,128]{3,2,1,0:T(8,128)S(1)}, u32[]{:S(2)}, u32[]{:S(2)}) collective-permute-start(s32[2,16,24,128]{3,2,1,0:T(8,128)S(1)} %pad_add_fusion.piece_ref), channel_id=1, source_target_pairs={{0,32},{1,33},{2,34},{3,35},{4,36},{5,37},{6,38},{7,39},{8,40},{9,... | collective-permute-start | bytes 1179656 | tf_op jit(solution)/shard_map/ppermute | solution.py:26
  39.6 18.2 %collective-permute-start.2 = (s32[2,16,24,128]{3,2,1,0:T(8,128)S(1)}, s32[2,16,24,128]{3,2,1,0:T(8,128)S(1)}, u32[]{:S(2)}, u32[]{:S(2)}) collective-permute-start(s32[2,16,24,128]{3,2,1,0:T(8,128)S(1)} %pad_add_fusion.piece_ref), channel_id=1, source_target_pairs={{0,16},{1,17},{2,18},{3,19},{4,20},{5,21},{6,22},{7,23},{8,24},{9,... | collective-permute-start | bytes 1179656 | tf_op jit(solution)/shard_map/ppermute | solution.py:26
  56.4 18.3 %collective-permute-start.6 = (f32[2,16,32,128]{3,2,1,0:T(8,128)S(1)}, f32[2,16,32,128]{3,2,1,0:T(8,128)}, u32[]{:S(2)}, u32[]{:S(2)}) collective-permute-start(f32[2,16,32,128]{3,2,1,0:T(8,128)S(1)} %pad_maximum_fusion.refs_7_.refs_15_), channel_id=1, source_target_pairs={{0,4},{1,5},{2,6},{3,7},{4,0},{5,1},{6,2},{7,3},{8,12},{9,13},{10,... | collective-permute-start | bytes 1572872 | tf_op jit(solution)/shard_map/ppermute | solution.py:26
  78.2 23.6 %collective-permute-start.15 = (s32[2,40,1024]{2,1,0:T(8,128)S(1)}, s32[2,40,1024]{2,1,0:T(8,128)S(1)}, u32[]{:S(2)}, u32[]{:S(2)}) collective-permute-start(s32[2,40,1024]{2,1,0:T(8,128)S(1)} %pad_add_fusion.1.refs_23_.refs_31_), channel_id=1, source_target_pairs={{0,12},{1,13},{2,14},{3,15},{4,8},{5,9},{6,10},{7,11},{8,4},{9,5},... | collective-permute-start | bytes 983048 | tf_op jit(solution)/shard_map/ppermute | solution.py:26
  80.0 21.8 %collective-permute-start.14 = (s32[2,40,1024]{2,1,0:T(8,128)S(1)}, s32[2,40,1024]{2,1,0:T(8,128)S(1)}, u32[]{:S(2)}, u32[]{:S(2)}) collective-permute-start(s32[2,40,1024]{2,1,0:T(8,128)S(1)} %pad_add_fusion.1.refs_23_.refs_31_), channel_id=1, source_target_pairs={{0,8},{1,9},{2,10},{3,11},{4,12},{5,13},{6,14},{7,15},{8,0},{9,1},... | collective-permute-start | bytes 983048 | tf_op jit(solution)/shard_map/ppermute | solution.py:26
  80.7 21.1 %collective-permute-start.13 = (s32[2,40,1024]{2,1,0:T(8,128)S(1)}, s32[2,40,1024]{2,1,0:T(8,128)S(1)}, u32[]{:S(2)}, u32[]{:S(2)}) collective-permute-start(s32[2,40,1024]{2,1,0:T(8,128)S(1)} %pad_add_fusion.1.refs_23_.refs_31_), channel_id=1, source_target_pairs={{0,4},{1,5},{2,6},{3,7},{4,0},{5,1},{6,2},{7,3},{8,12},{9,13},{10,... | collective-permute-start | bytes 983048 | tf_op jit(solution)/shard_map/ppermute | solution.py:26
  103.2 44.1 %collective-permute-start.30 = (s32[2,40,1024]{2,1,0:T(8,128)S(1)}, s32[2,40,1024]{2,1,0:T(8,128)S(1)}, u32[]{:S(2)}, u32[]{:S(2)}) collective-permute-start(s32[2,40,1024]{2,1,0:T(8,128)S(1)} %pad_add_fusion.1.refs_23_.refs_31_), channel_id=1, source_target_pairs={{0,1},{1,0},{2,3},{3,2},{4,5},{5,4},{6,7},{7,6},{8,9},{9,8},{10,11... | collective-permute-start | bytes 983048 | tf_op jit(solution)/shard_map/ppermute | solution.py:26
  103.3 52.9 %collective-permute-start.31 = (s32[2,40,1024]{2,1,0:T(8,128)S(1)}, s32[2,40,1024]{2,1,0:T(8,128)S(1)}, u32[]{:S(2)}, u32[]{:S(2)}) collective-permute-start(s32[2,40,1024]{2,1,0:T(8,128)S(1)} %collective-permute-done.13.refs_24_.refs_32_), channel_id=1, source_target_pairs={{0,1},{1,0},{2,3},{3,2},{4,5},{5,4},{6,7},{7,6},{8,9},{9,8},{10,11... | collective-permute-start | bytes 983048 | tf_op jit(solution)/shard_map/ppermute | solution.py:26
  108.2 7.5 %collective-permute-start.17 = (f32[64,512]{1,0:T(8,128)S(1)}, f32[64,512]{1,0:T(8,128)S(1)}, u32[]{:S(2)}, u32[]{:S(2)}) collective-permute-start(f32[64,512]{1,0:T(8,128)S(1)} %get-tuple-element.62), channel_id=1, source_target_pairs={{0,8},{1,9},{2,10},{3,11},{4,12},{5,13},{6,14},{7,15},{8,0},{9,1},... | collective-permute-start | bytes 393224 | tf_op jit(solution)/shard_map/ppermute | solution.py:26
  128.2 17.1 %collective-permute-start.24 = (f32[64,512]{1,0:T(8,128)S(1)}, f32[64,512]{1,0:T(8,128)S(1)}, u32[]{:S(2)}, u32[]{:S(2)}) collective-permute-start(f32[64,512]{1,0:T(8,128)S(1)} %add_add_fusion.3), channel_id=1, source_target_pairs={{0,16},{1,17},{2,18},{3,19},{4,20},{5,21},{6,22},{7,23},{8,24},{9,... | collective-permute-start | bytes 393224 | tf_op jit(solution)/shard_map/ppermute | solution.py:26
  128.2 17.1 %collective-permute-start.23 = (f32[64,512]{1,0:T(8,128)S(1)}, f32[64,512]{1,0:T(8,128)S(1)}, u32[]{:S(2)}, u32[]{:S(2)}) collective-permute-start(f32[64,512]{1,0:T(8,128)S(1)} %add_add_fusion.3), channel_id=1, source_target_pairs={{0,32},{1,33},{2,34},{3,35},{4,36},{5,37},{6,38},{7,39},{8,40},{9,... | collective-permute-start | bytes 393224 | tf_op jit(solution)/shard_map/ppermute | solution.py:26
  130.6 25.5 %collective-permute-start.32 = (s32[2,40,1024]{2,1,0:T(8,128)S(1)}, s32[2,40,1024]{2,1,0:T(8,128)S(1)}, u32[]{:S(2)}, u32[]{:S(2)}) collective-permute-start(s32[2,40,1024]{2,1,0:T(8,128)S(1)} %collective-permute-done.14.refs_25_.refs_33_), channel_id=1, source_target_pairs={{0,1},{1,0},{2,3},{3,2},{4,5},{5,4},{6,7},{7,6},{8,9},{9,8},{10,11... | collective-permute-start | bytes 983048 | tf_op jit(solution)/shard_map/ppermute | solution.py:26
  145.4 8.7 %collective-permute-start.28 = (f32[64,512]{1,0:T(8,128)S(1)}, f32[64,512]{1,0:T(8,128)S(1)}, u32[]{:S(2)}, u32[]{:S(2)}) collective-permute-start(f32[64,512]{1,0:T(8,128)S(1)} %add_add_fusion.2), channel_id=1, source_target_pairs={{0,12},{1,13},{2,14},{3,15},{4,8},{5,9},{6,10},{7,11},{8,4},{9,5},... | collective-permute-start | bytes 393224 | tf_op jit(solution)/shard_map/ppermute | solution.py:26
  147.2 8.1 %collective-permute-start.27 = (f32[64,512]{1,0:T(8,128)S(1)}, f32[64,512]{1,0:T(8,128)S(1)}, u32[]{:S(2)}, u32[]{:S(2)}) collective-permute-start(f32[64,512]{1,0:T(8,128)S(1)} %add_add_fusion.2), channel_id=1, source_target_pairs={{0,8},{1,9},{2,10},{3,11},{4,12},{5,13},{6,14},{7,15},{8,0},{9,1},... | collective-permute-start | bytes 393224 | tf_op jit(solution)/shard_map/ppermute | solution.py:26
  147.2 8.1 %collective-permute-start.26 = (f32[64,512]{1,0:T(8,128)S(1)}, f32[64,512]{1,0:T(8,128)S(1)}, u32[]{:S(2)}, u32[]{:S(2)}) collective-permute-start(f32[64,512]{1,0:T(8,128)S(1)} %add_add_fusion.2), channel_id=1, source_target_pairs={{0,4},{1,5},{2,6},{3,7},{4,0},{5,1},{6,2},{7,3},{8,12},{9,13},{10,... | collective-permute-start | bytes 393224 | tf_op jit(solution)/shard_map/ppermute | solution.py:26
  184.0 7.8 %collective-permute-start.35 = (f32[64,512]{1,0:T(8,128)S(1)}, f32[64,512]{1,0:T(8,128)S(1)}, u32[]{:S(2)}, u32[]{:S(2)}) collective-permute-start(f32[64,512]{1,0:T(8,128)S(1)} %get-tuple-element.59), channel_id=1, source_target_pairs={{0,8},{1,9},{2,10},{3,11},{4,12},{5,13},{6,14},{7,15},{8,0},{9,1},... | collective-permute-start | bytes 393224 | tf_op jit(solution)/shard_map/ppermute | solution.py:26
  215.4 7.4 %collective-permute-start.47 = (f32[256,512]{1,0:T(8,128)S(1)}, f32[256,512]{1,0:T(8,128)S(1)}, u32[]{:S(2)}, u32[]{:S(2)}) collective-permute-start(f32[256,512]{1,0:T(8,128)S(1)} %pad_maximum_fusion.2.near1_ref), channel_id=1, source_target_pairs={{0,1},{1,0},{2,3},{3,2},{4,5},{5,4},{6,7},{7,6},{8,9},{9,8},{10,11... | collective-permute-start | bytes 1572872 | tf_op jit(solution)/shard_map/ppermute | solution.py:26
  (46 other events, 480.5 us)
